TPU v7x, 256 devices: a whole 4x4x8 slice. The times are simulated.
256 devices in a mesh: blk: 64 (over z, y, x_hi), rep: 4 (over x_lo, core).
Axes of the slice: x: 4 (x_hi: 2, x_lo: 2; x = x_hi * 2 + x_lo), y: 4, z: 8, core: 2. Of those that a mesh axis runs over, the one named last changes fastest.
Arguments:
- cotangent: bfloat16 [65536, 256], P('blk'), may hold values from -6 to 6
- features: bfloat16 [65536, 768], P('blk', 'rep'), may hold values from -6 to 6
- weight: bfloat16 [768, 256], P('rep'), may hold values from -0.375 to 0.375
- heat_time: float32 [1], replicated, may hold values from 0.5 to 4
- tile_values: bfloat16 [4096, 256, 256], P(('blk', 'rep')), may hold values from -0.09375 to 0.09375
- tile_row: int32 [4096], P(('blk', 'rep')), may hold values from 0 to 255, as said below
- tile_col: int32 [4096], P(('blk', 'rep')), may hold values from 0 to 255, as said below
- section_offsets: int32 [4352], P(('blk', 'rep')), may hold values from 0 to 16, as said below
Outputs:
- grad_weight: float32 [768, 256], P('rep')
- grad_features: bfloat16 [65536, 768], P('blk', 'rep')
Inputs may be any that keep to these rules, and one draw needn't show every extreme that they name: `tile_row`: for the device at blk index d and rep index r, the live slots between its offsets m and m + 1 (m = 0 to 15) name row tiles of node block (d - r - 4 * m) mod 64, that is row tiles (4 blocks further back for each m) of that block's 4 tiles; slots past the last offset are unused. `tile_col`: every live slot of the device at blk index d names a column tile of node block d. `section_offsets`: each device's 16 + 1 offsets start at 0 and never fall; the last one is its count of live slots, which differs between devices, and is 16 on at least one device.
All inputs are finite; a program needn't handle non-finite values.
Results may differ from a plain program's by a relative error of at most 0.0053.
Values may be sent and summed in bfloat16 or wider, within the bound.
A program may use at most 64 MiB of HBM per device.

v0:
```python
import math

import jax
import jax.numpy as jnp
from jax import lax
from jax.sharding import PartitionSpec as P


def shifted(value, axis, by):
    length = lax.axis_size(axis)
    return lax.ppermute(value, axis, [(i, (i + by) % length) for i in range(length)])


def taylor_coef(heat_time):
    tvalue = heat_time[0]
    taylor = jnp.stack([jnp.ones((), jnp.float32), tvalue, tvalue * tvalue / 2.0])
    return taylor / jnp.sum(taylor)


def local(cotangent, features, weight, heat_time, tile_values, tile_row, tile_col, section_offsets):
    block_count = lax.axis_size("blk")
    copy_count = lax.axis_size("rep")
    section_count = block_count // copy_count
    node_rows = cotangent.shape[0]
    width = cotangent.shape[1]
    tile_size = tile_values.shape[1]
    slot_count = tile_values.shape[0]
    tiles_here = node_rows // tile_size
    my_block = lax.axis_index("blk")
    my_copy = lax.axis_index("rep")
    local_row = tile_row % tiles_here
    local_col = tile_col - my_block * tiles_here
    slot_index = jnp.arange(slot_count, dtype=jnp.int32)
    inner_cuts = section_offsets[1:section_count]
    slot_section = jnp.sum((slot_index[:, None] >= inner_cuts[None, :]).astype(jnp.int32), axis=1)
    alive_mask = (slot_index < section_offsets[section_count]).astype(jnp.float32)
    pick_index = slot_section * tiles_here + local_row
    target_table = (jnp.arange(tiles_here, dtype=jnp.int32)[:, None] == local_col[None, :]).astype(
        jnp.float32
    )
    target_table = target_table * alive_mask[None, :]

    def absorb(stacked):
        flat_blocks = stacked.reshape(section_count * tiles_here, tile_size, width)
        picked = jnp.take(flat_blocks, pick_index, axis=0)
        terms = jnp.einsum("kab,kac->kbc", tile_values, picked, preferred_element_type=jnp.float32)
        summed = jnp.dot(
            target_table,
            terms.reshape(slot_count, tile_size * width),
            precision=lax.Precision.HIGHEST,
            preferred_element_type=jnp.float32,
        )
        return summed.reshape(node_rows, width)

    def propagate(field):
        current = field
        for bit_pos in range(copy_count.bit_length() - 1):
            moved = shifted(current, "blk", 1 << bit_pos)
            current = jnp.where(my_copy >> bit_pos & 1 == 1, moved, current)
        stacked = jnp.zeros((section_count, node_rows, width), field.dtype)
        stacked = lax.dynamic_update_index_in_dim(stacked, current, 0, 0)

        def advance(section_idx, state_pair):
            source_block, holder = state_pair
            source_block = shifted(source_block, "blk", copy_count)
            return (
                source_block,
                lax.dynamic_update_index_in_dim(holder, source_block, section_idx, 0),
            )

        _, stacked = lax.fori_loop(1, section_count, advance, (current, stacked))
        return absorb(stacked)

    partial_first = propagate(cotangent)
    first = lax.psum(partial_first, "rep").astype(jnp.bfloat16)
    second = lax.psum(propagate(first), "rep")
    coef = taylor_coef(heat_time)
    combined = (
        coef[0] * cotangent.astype(jnp.float32)
        + coef[1] * first.astype(jnp.float32)
        + coef[2] * second
    )
    combined = combined.astype(jnp.bfloat16)
    grad_features = lax.dot_general(
        combined, weight, (((1,), (1,)), ((), ())), preferred_element_type=jnp.float32
    ).astype(jnp.bfloat16)
    node_total = node_rows * block_count
    partial_weight = lax.dot_general(
        features, combined, (((0,), (0,)), ((), ())), preferred_element_type=jnp.float32
    ) * (1.0 / math.sqrt(node_total))
    grad_weight = lax.psum(partial_weight, "blk")
    return (grad_weight, grad_features)


def solution(mesh):
    in_specs = (
        P("blk", None),
        P("blk", "rep"),
        P("rep", None),
        P(),
        P(("blk", "rep"), None, None),
        P(("blk", "rep")),
        P(("blk", "rep")),
        P(("blk", "rep")),
    )
    out_specs = (P("rep", None), P("blk", "rep"))
    return jax.shard_map(local, mesh=mesh, in_specs=in_specs, out_specs=out_specs, check_vma=False)
```

profile of v0, /device:TPU:2, one launch (start us, length us, event | category | flops | bytes accessed | tf_op | source)
XLA Modules:
  0.0 1347.0 jit_solution(16071397794665211176)
XLA Ops:
  12.2 17.1 %collective-permute-done.2 = bf16[1024,256]{1,0:T(8,128)(2,1)S(1)} collective-permute-done((bf16[1024,256]{1,0:T(8,128)(2,1)}, bf16[1024,256]{1,0:T(8,128)(2,1)S(1)}, u32[]{:S(2)}, u32[]{:S(2)}) %collective-permute-start.2) | collective-permute-done | bytes 524320 | tf_op jit(solution)/shard_map/ppermute | solution.py:11
  50.0 238.8 %while.30 = (s32[]{:T(128)}, bf16[1024,256]{1,0:T(8,128)(2,1)S(1)}, bf16[16,1024,256]{2,1,0:T(8,128)(2,1)}, s32[]{:T(128)}, s32[]{:T(128)}, /*index=5*/s32[]{:T(128)}) while((s32[]{:T(128)}, bf16[1024,256]{1,0:T(8,128)(2,1)S(1)}, bf16[16,1024,256]{2,1,0:T(8,128)(2,1)}, s32[]{:T(128)}, s32[]{:T(128)}, /*index=5*/s32[]{:T(128)}) %tuple.59), condition=%wide.region_1.2_spmd, body=%wide.region_0.1_spmd.sunk | while | flops 5 | bytes 4194459 | solution.py:71
  50.0 14.8 %collective-permute-done = bf16[1024,256]{1,0:T(8,128)(2,1)S(1)} collective-permute-done((bf16[1024,256]{1,0:T(8,128)(2,1)S(1)}, bf16[1024,256]{1,0:T(8,128)(2,1)S(1)}, u32[]{:S(2)}, u32[]{:S(2)}) %collective-permute-start) | collective-permute-done | bytes 524320 | tf_op jit(solution)/shard_map/while/body/eval_jaxpr/ppermute | solution.py:11
  137.4 15.6 %collective-permute-done = bf16[1024,256]{1,0:T(8,128)(2,1)S(1)} collective-permute-done((bf16[1024,256]{1,0:T(8,128)(2,1)S(1)}, bf16[1024,256]{1,0:T(8,128)(2,1)S(1)}, u32[]{:S(2)}, u32[]{:S(2)}) %collective-permute-start) | collective-permute-done | bytes 524320 | tf_op jit(solution)/shard_map/while/body/eval_jaxpr/ppermute | solution.py:11
  153.9 16.6 %collective-permute-done = bf16[1024,256]{1,0:T(8,128)(2,1)S(1)} collective-permute-done((bf16[1024,256]{1,0:T(8,128)(2,1)S(1)}, bf16[1024,256]{1,0:T(8,128)(2,1)S(1)}, u32[]{:S(2)}, u32[]{:S(2)}) %collective-permute-start) | collective-permute-done | bytes 524320 | tf_op jit(solution)/shard_map/while/body/eval_jaxpr/ppermute | solution.py:11
  171.4 17.8 %collective-permute-done = bf16[1024,256]{1,0:T(8,128)(2,1)S(1)} collective-permute-done((bf16[1024,256]{1,0:T(8,128)(2,1)S(1)}, bf16[1024,256]{1,0:T(8,128)(2,1)S(1)}, u32[]{:S(2)}, u32[]{:S(2)}) %collective-permute-start) | collective-permute-done | bytes 524320 | tf_op jit(solution)/shard_map/while/body/eval_jaxpr/ppermute | solution.py:11
  190.1 17.9 %collective-permute-done = bf16[1024,256]{1,0:T(8,128)(2,1)S(1)} collective-permute-done((bf16[1024,256]{1,0:T(8,128)(2,1)S(1)}, bf16[1024,256]{1,0:T(8,128)(2,1)S(1)}, u32[]{:S(2)}, u32[]{:S(2)}) %collective-permute-start) | collective-permute-done | bytes 524320 | tf_op jit(solution)/shard_map/while/body/eval_jaxpr/ppermute | solution.py:11
  208.9 17.1 %collective-permute-done = bf16[1024,256]{1,0:T(8,128)(2,1)S(1)} collective-permute-done((bf16[1024,256]{1,0:T(8,128)(2,1)S(1)}, bf16[1024,256]{1,0:T(8,128)(2,1)S(1)}, u32[]{:S(2)}, u32[]{:S(2)}) %collective-permute-start) | collective-permute-done | bytes 524320 | tf_op jit(solution)/shard_map/while/body/eval_jaxpr/ppermute | solution.py:11
  226.8 16.2 %collective-permute-done = bf16[1024,256]{1,0:T(8,128)(2,1)S(1)} collective-permute-done((bf16[1024,256]{1,0:T(8,128)(2,1)S(1)}, bf16[1024,256]{1,0:T(8,128)(2,1)S(1)}, u32[]{:S(2)}, u32[]{:S(2)}) %collective-permute-start) | collective-permute-done | bytes 524320 | tf_op jit(solution)/shard_map/while/body/eval_jaxpr/ppermute | solution.py:11
  243.8 15.2 %collective-permute-done = bf16[1024,256]{1,0:T(8,128)(2,1)S(1)} collective-permute-done((bf16[1024,256]{1,0:T(8,128)(2,1)S(1)}, bf16[1024,256]{1,0:T(8,128)(2,1)S(1)}, u32[]{:S(2)}, u32[]{:S(2)}) %collective-permute-start) | collective-permute-done | bytes 524320 | tf_op jit(solution)/shard_map/while/body/eval_jaxpr/ppermute | solution.py:11
  310.1 25.9 %all-reduce.9 = bf16[1024,256]{1,0:T(8,128)(2,1)S(1)} all-reduce(f32[1024,256]{1,0:T(8,128)} %reshape.47), channel_id=1, replica_groups=mesh['blk'=64,'rep'=4] {'rep'}, use_global_device_ids=true, to_apply=%region_3.5 | all-reduce | flops 262144 | bytes 1572864 | tf_op jit(solution)/shard_map/psum | solution.py:75
  336.0 20.0 %collective-permute-done.4 = bf16[1024,256]{1,0:T(8,128)(2,1)S(1)} collective-permute-done((bf16[1024,256]{1,0:T(8,128)(2,1)S(1)}, bf16[1024,256]{1,0:T(8,128)(2,1)S(1)}, u32[]{:S(2)}, u32[]{:S(2)}) %collective-permute-start.4) | collective-permute-done | bytes 524320 | tf_op jit(solution)/shard_map/ppermute | solution.py:11
  356.3 16.9 %collective-permute-done.5 = bf16[1024,256]{1,0:T(8,128)(2,1)} collective-permute-done((bf16[1024,256]{1,0:T(8,128)(2,1)S(1)}, bf16[1024,256]{1,0:T(8,128)(2,1)}, u32[]{:S(2)}, u32[]{:S(2)}) %collective-permute-start.5) | collective-permute-done | bytes 524320 | tf_op jit(solution)/shard_map/ppermute | solution.py:11
  378.4 254.1 %while.31 = (s32[]{:T(128)}, bf16[1024,256]{1,0:T(8,128)(2,1)}, bf16[16,1024,256]{2,1,0:T(8,128)(2,1)}, s32[]{:T(128)}, s32[]{:T(128)}, /*index=5*/s32[]{:T(128)}) while((s32[]{:T(128)}, bf16[1024,256]{1,0:T(8,128)(2,1)}, bf16[16,1024,256]{2,1,0:T(8,128)(2,1)}, s32[]{:T(128)}, s32[]{:T(128)}, /*index=5*/s32[]{:T(128)}) %tuple.70), condition=%wide.region_5.7_spmd, body=%wide.region_4.6_spmd.sunk | while | flops 5 | bytes 4194459 | solution.py:71
  378.4 16.4 %collective-permute-done.1 = bf16[1024,256]{1,0:T(8,128)(2,1)S(1)} collective-permute-done((bf16[1024,256]{1,0:T(8,128)(2,1)}, bf16[1024,256]{1,0:T(8,128)(2,1)S(1)}, u32[]{:S(2)}, u32[]{:S(2)}) %collective-permute-start.1) | collective-permute-done | bytes 524320 | tf_op jit(solution)/shard_map/while/body/eval_jaxpr/ppermute | solution.py:11
  396.4 15.5 %collective-permute-done.1 = bf16[1024,256]{1,0:T(8,128)(2,1)S(1)} collective-permute-done((bf16[1024,256]{1,0:T(8,128)(2,1)}, bf16[1024,256]{1,0:T(8,128)(2,1)S(1)}, u32[]{:S(2)}, u32[]{:S(2)}) %collective-permute-start.1) | collective-permute-done | bytes 524320 | tf_op jit(solution)/shard_map/while/body/eval_jaxpr/ppermute | solution.py:11
  505.4 15.4 %collective-permute-done.1 = bf16[1024,256]{1,0:T(8,128)(2,1)S(1)} collective-permute-done((bf16[1024,256]{1,0:T(8,128)(2,1)}, bf16[1024,256]{1,0:T(8,128)(2,1)S(1)}, u32[]{:S(2)}, u32[]{:S(2)}) %collective-permute-start.1) | collective-permute-done | bytes 524320 | tf_op jit(solution)/shard_map/while/body/eval_jaxpr/ppermute | solution.py:11
  522.4 16.5 %collective-permute-done.1 = bf16[1024,256]{1,0:T(8,128)(2,1)S(1)} collective-permute-done((bf16[1024,256]{1,0:T(8,128)(2,1)}, bf16[1024,256]{1,0:T(8,128)(2,1)S(1)}, u32[]{:S(2)}, u32[]{:S(2)}) %collective-permute-start.1) | collective-permute-done | bytes 524320 | tf_op jit(solution)/shard_map/while/body/eval_jaxpr/ppermute | solution.py:11
  540.6 17.6 %collective-permute-done.1 = bf16[1024,256]{1,0:T(8,128)(2,1)S(1)} collective-permute-done((bf16[1024,256]{1,0:T(8,128)(2,1)}, bf16[1024,256]{1,0:T(8,128)(2,1)S(1)}, u32[]{:S(2)}, u32[]{:S(2)}) %collective-permute-start.1) | collective-permute-done | bytes 524320 | tf_op jit(solution)/shard_map/while/body/eval_jaxpr/ppermute | solution.py:11
  559.9 18.5 %collective-permute-done.1 = bf16[1024,256]{1,0:T(8,128)(2,1)S(1)} collective-permute-done((bf16[1024,256]{1,0:T(8,128)(2,1)}, bf16[1024,256]{1,0:T(8,128)(2,1)S(1)}, u32[]{:S(2)}, u32[]{:S(2)}) %collective-permute-start.1) | collective-permute-done | bytes 524320 | tf_op jit(solution)/shard_map/while/body/eval_jaxpr/ppermute | solution.py:11
  580.1 17.6 %collective-permute-done.1 = bf16[1024,256]{1,0:T(8,128)(2,1)S(1)} collective-permute-done((bf16[1024,256]{1,0:T(8,128)(2,1)}, bf16[1024,256]{1,0:T(8,128)(2,1)S(1)}, u32[]{:S(2)}, u32[]{:S(2)}) %collective-permute-start.1) | collective-permute-done | bytes 524320 | tf_op jit(solution)/shard_map/while/body/eval_jaxpr/ppermute | solution.py:11
  599.3 16.7 %collective-permute-done.1 = bf16[1024,256]{1,0:T(8,128)(2,1)S(1)} collective-permute-done((bf16[1024,256]{1,0:T(8,128)(2,1)}, bf16[1024,256]{1,0:T(8,128)(2,1)S(1)}, u32[]{:S(2)}, u32[]{:S(2)}) %collective-permute-start.1) | collective-permute-done | bytes 524320 | tf_op jit(solution)/shard_map/while/body/eval_jaxpr/ppermute | solution.py:11
  657.4 40.3 %all-reduce.6.cloned.1.call-done = f32[1024,256]{1,0:T(8,128)} async-done(((f32[1024,256]{1,0:T(8,128)}), f32[1024,256]{1,0:T(8,128)}) %all-reduce.6.cloned.1.call-update) | async-done | bytes 1048592 | tf_op jit(solution)/shard_map/psum | solution.py:76
  704.3 634.2 %all-reduce.8.cloned.1.call-done = f32[192,256]{1,0:T(8,128)} async-done(((f32[192,256]{1,0:T(8,128)}), f32[192,256]{1,0:T(8,128)}) %all-reduce.8.cloned.1.call-update) | async-done | bytes 196624 | tf_op jit(solution)/shard_map/psum | solution.py:91
  (148 shorter events, 312.3 us)
Async XLA Ops:
  7.2 690.6 %all-reduce.6.cloned.1.call-start = ((), (), s32[]{:S(2)}) async-start(), calls=%async_computation | async-start | bytes 2097152 | tf_op jit(solution)/shard_map/psum | solution.py:76
  7.2 22.1 %collective-permute-start.2 = (bf16[1024,256]{1,0:T(8,128)(2,1)}, bf16[1024,256]{1,0:T(8,128)(2,1)S(1)}, u32[]{:S(2)}, u32[]{:S(2)}) collective-permute-start(bf16[1024,256]{1,0:T(8,128)(2,1)} %param.14), channel_id=1, source_target_pairs={{0,4},{4,8},{8,12},{12,16},{16,20},{20,24},{24,28},{28,32},{32,36}... | collective-permute-start | bytes 1572872 | tf_op jit(solution)/shard_map/ppermute | solution.py:11
  30.4 15.5 %collective-permute-start.3 = (bf16[1024,256]{1,0:T(8,128)(2,1)S(1)}, bf16[1024,256]{1,0:T(8,128)(2,1)S(1)}, u32[]{:S(2)}, u32[]{:S(2)}) collective-permute-start(bf16[1024,256]{1,0:T(8,128)(2,1)S(1)} %broadcast_select_fusion.1), channel_id=1, source_target_pairs={{0,8},{4,12},{8,16},{12,20},{16,24},{20,28},{24,32},{28,36},{32,40... | collective-permute-start | bytes 1572872 | tf_op jit(solution)/shard_map/ppermute | solution.py:11
  50.0 14.8 %collective-permute-start = (bf16[1024,256]{1,0:T(8,128)(2,1)S(1)}, bf16[1024,256]{1,0:T(8,128)(2,1)S(1)}, u32[]{:S(2)}, u32[]{:S(2)}) collective-permute-start(bf16[1024,256]{1,0:T(8,128)(2,1)S(1)} %get-tuple-element.195), channel_id=1, source_target_pairs={{0,16},{4,20},{8,24},{12,28},{16,32},{20,36},{24,40},{28,44},{32,4... | collective-permute-start | bytes 1572872 | tf_op jit(solution)/shard_map/while/body/eval_jaxpr/ppermute | solution.py:11
  122.1 14.5 %collective-permute-start = (bf16[1024,256]{1,0:T(8,128)(2,1)S(1)}, bf16[1024,256]{1,0:T(8,128)(2,1)S(1)}, u32[]{:S(2)}, u32[]{:S(2)}) collective-permute-start(bf16[1024,256]{1,0:T(8,128)(2,1)S(1)} %get-tuple-element.195), channel_id=1, source_target_pairs={{0,16},{4,20},{8,24},{12,28},{16,32},{20,36},{24,40},{28,44},{32,4... | collective-permute-start | bytes 1572872 | tf_op jit(solution)/shard_map/while/body/eval_jaxpr/ppermute | solution.py:11
  137.4 15.6 %collective-permute-start = (bf16[1024,256]{1,0:T(8,128)(2,1)S(1)}, bf16[1024,256]{1,0:T(8,128)(2,1)S(1)}, u32[]{:S(2)}, u32[]{:S(2)}) collective-permute-start(bf16[1024,256]{1,0:T(8,128)(2,1)S(1)} %get-tuple-element.195), channel_id=1, source_target_pairs={{0,16},{4,20},{8,24},{12,28},{16,32},{20,36},{24,40},{28,44},{32,4... | collective-permute-start | bytes 1572872 | tf_op jit(solution)/shard_map/while/body/eval_jaxpr/ppermute | solution.py:11
  153.9 16.6 %collective-permute-start = (bf16[1024,256]{1,0:T(8,128)(2,1)S(1)}, bf16[1024,256]{1,0:T(8,128)(2,1)S(1)}, u32[]{:S(2)}, u32[]{:S(2)}) collective-permute-start(bf16[1024,256]{1,0:T(8,128)(2,1)S(1)} %get-tuple-element.195), channel_id=1, source_target_pairs={{0,16},{4,20},{8,24},{12,28},{16,32},{20,36},{24,40},{28,44},{32,4... | collective-permute-start | bytes 1572872 | tf_op jit(solution)/shard_map/while/body/eval_jaxpr/ppermute | solution.py:11
  171.4 17.8 %collective-permute-start = (bf16[1024,256]{1,0:T(8,128)(2,1)S(1)}, bf16[1024,256]{1,0:T(8,128)(2,1)S(1)}, u32[]{:S(2)}, u32[]{:S(2)}) collective-permute-start(bf16[1024,256]{1,0:T(8,128)(2,1)S(1)} %get-tuple-element.195), channel_id=1, source_target_pairs={{0,16},{4,20},{8,24},{12,28},{16,32},{20,36},{24,40},{28,44},{32,4... | collective-permute-start | bytes 1572872 | tf_op jit(solution)/shard_map/while/body/eval_jaxpr/ppermute | solution.py:11
  190.1 17.9 %collective-permute-start = (bf16[1024,256]{1,0:T(8,128)(2,1)S(1)}, bf16[1024,256]{1,0:T(8,128)(2,1)S(1)}, u32[]{:S(2)}, u32[]{:S(2)}) collective-permute-start(bf16[1024,256]{1,0:T(8,128)(2,1)S(1)} %get-tuple-element.195), channel_id=1, source_target_pairs={{0,16},{4,20},{8,24},{12,28},{16,32},{20,36},{24,40},{28,44},{32,4... | collective-permute-start | bytes 1572872 | tf_op jit(solution)/shard_map/while/body/eval_jaxpr/ppermute | solution.py:11
  208.9 17.1 %collective-permute-start = (bf16[1024,256]{1,0:T(8,128)(2,1)S(1)}, bf16[1024,256]{1,0:T(8,128)(2,1)S(1)}, u32[]{:S(2)}, u32[]{:S(2)}) collective-permute-start(bf16[1024,256]{1,0:T(8,128)(2,1)S(1)} %get-tuple-element.195), channel_id=1, source_target_pairs={{0,16},{4,20},{8,24},{12,28},{16,32},{20,36},{24,40},{28,44},{32,4... | collective-permute-start | bytes 1572872 | tf_op jit(solution)/shard_map/while/body/eval_jaxpr/ppermute | solution.py:11
  226.8 16.2 %collective-permute-start = (bf16[1024,256]{1,0:T(8,128)(2,1)S(1)}, bf16[1024,256]{1,0:T(8,128)(2,1)S(1)}, u32[]{:S(2)}, u32[]{:S(2)}) collective-permute-start(bf16[1024,256]{1,0:T(8,128)(2,1)S(1)} %get-tuple-element.195), channel_id=1, source_target_pairs={{0,16},{4,20},{8,24},{12,28},{16,32},{20,36},{24,40},{28,44},{32,4... | collective-permute-start | bytes 1572872 | tf_op jit(solution)/shard_map/while/body/eval_jaxpr/ppermute | solution.py:11
  243.8 15.2 %collective-permute-start = (bf16[1024,256]{1,0:T(8,128)(2,1)S(1)}, bf16[1024,256]{1,0:T(8,128)(2,1)S(1)}, u32[]{:S(2)}, u32[]{:S(2)}) collective-permute-start(bf16[1024,256]{1,0:T(8,128)(2,1)S(1)} %get-tuple-element.195), channel_id=1, source_target_pairs={{0,16},{4,20},{8,24},{12,28},{16,32},{20,36},{24,40},{28,44},{32,4... | collective-permute-start | bytes 1572872 | tf_op jit(solution)/shard_map/while/body/eval_jaxpr/ppermute | solution.py:11
  335.9 20.1 %collective-permute-start.4 = (bf16[1024,256]{1,0:T(8,128)(2,1)S(1)}, bf16[1024,256]{1,0:T(8,128)(2,1)S(1)}, u32[]{:S(2)}, u32[]{:S(2)}) collective-permute-start(bf16[1024,256]{1,0:T(8,128)(2,1)S(1)} %all-reduce.9), channel_id=1, source_target_pairs={{0,4},{4,8},{8,12},{12,16},{16,20},{20,24},{24,28},{28,32},{32,36}... | collective-permute-start | bytes 1572872 | tf_op jit(solution)/shard_map/ppermute | solution.py:11
  356.0 17.2 %collective-permute-start.5 = (bf16[1024,256]{1,0:T(8,128)(2,1)S(1)}, bf16[1024,256]{1,0:T(8,128)(2,1)}, u32[]{:S(2)}, u32[]{:S(2)}) collective-permute-start(bf16[1024,256]{1,0:T(8,128)(2,1)S(1)} %broadcast_select_fusion), channel_id=1, source_target_pairs={{0,8},{4,12},{8,16},{12,20},{16,24},{20,28},{24,32},{28,36},{32,40... | collective-permute-start | bytes 1572872 | tf_op jit(solution)/shard_map/ppermute | solution.py:11
  378.4 16.4 %collective-permute-start.1 = (bf16[1024,256]{1,0:T(8,128)(2,1)}, bf16[1024,256]{1,0:T(8,128)(2,1)S(1)}, u32[]{:S(2)}, u32[]{:S(2)}) collective-permute-start(bf16[1024,256]{1,0:T(8,128)(2,1)} %get-tuple-element.213), channel_id=1, source_target_pairs={{0,16},{4,20},{8,24},{12,28},{16,32},{20,36},{24,40},{28,44},{32,4... | collective-permute-start | bytes 1572872 | tf_op jit(solution)/shard_map/while/body/eval_jaxpr/ppermute | solution.py:11
  396.4 15.5 %collective-permute-start.1 = (bf16[1024,256]{1,0:T(8,128)(2,1)}, bf16[1024,256]{1,0:T(8,128)(2,1)S(1)}, u32[]{:S(2)}, u32[]{:S(2)}) collective-permute-start(bf16[1024,256]{1,0:T(8,128)(2,1)} %get-tuple-element.213), channel_id=1, source_target_pairs={{0,16},{4,20},{8,24},{12,28},{16,32},{20,36},{24,40},{28,44},{32,4... | collective-permute-start | bytes 1572872 | tf_op jit(solution)/shard_map/while/body/eval_jaxpr/ppermute | solution.py:11
  413.6 14.6 %collective-permute-start.1 = (bf16[1024,256]{1,0:T(8,128)(2,1)}, bf16[1024,256]{1,0:T(8,128)(2,1)S(1)}, u32[]{:S(2)}, u32[]{:S(2)}) collective-permute-start(bf16[1024,256]{1,0:T(8,128)(2,1)} %get-tuple-element.213), channel_id=1, source_target_pairs={{0,16},{4,20},{8,24},{12,28},{16,32},{20,36},{24,40},{28,44},{32,4... | collective-permute-start | bytes 1572872 | tf_op jit(solution)/shard_map/while/body/eval_jaxpr/ppermute | solution.py:11
  505.4 15.4 %collective-permute-start.1 = (bf16[1024,256]{1,0:T(8,128)(2,1)}, bf16[1024,256]{1,0:T(8,128)(2,1)S(1)}, u32[]{:S(2)}, u32[]{:S(2)}) collective-permute-start(bf16[1024,256]{1,0:T(8,128)(2,1)} %get-tuple-element.213), channel_id=1, source_target_pairs={{0,16},{4,20},{8,24},{12,28},{16,32},{20,36},{24,40},{28,44},{32,4... | collective-permute-start | bytes 1572872 | tf_op jit(solution)/shard_map/while/body/eval_jaxpr/ppermute | solution.py:11
  522.4 16.5 %collective-permute-start.1 = (bf16[1024,256]{1,0:T(8,128)(2,1)}, bf16[1024,256]{1,0:T(8,128)(2,1)S(1)}, u32[]{:S(2)}, u32[]{:S(2)}) collective-permute-start(bf16[1024,256]{1,0:T(8,128)(2,1)} %get-tuple-element.213), channel_id=1, source_target_pairs={{0,16},{4,20},{8,24},{12,28},{16,32},{20,36},{24,40},{28,44},{32,4... | collective-permute-start | bytes 1572872 | tf_op jit(solution)/shard_map/while/body/eval_jaxpr/ppermute | solution.py:11
  540.6 17.6 %collective-permute-start.1 = (bf16[1024,256]{1,0:T(8,128)(2,1)}, bf16[1024,256]{1,0:T(8,128)(2,1)S(1)}, u32[]{:S(2)}, u32[]{:S(2)}) collective-permute-start(bf16[1024,256]{1,0:T(8,128)(2,1)} %get-tuple-element.213), channel_id=1, source_target_pairs={{0,16},{4,20},{8,24},{12,28},{16,32},{20,36},{24,40},{28,44},{32,4... | collective-permute-start | bytes 1572872 | tf_op jit(solution)/shard_map/while/body/eval_jaxpr/ppermute | solution.py:11
  559.9 18.5 %collective-permute-start.1 = (bf16[1024,256]{1,0:T(8,128)(2,1)}, bf16[1024,256]{1,0:T(8,128)(2,1)S(1)}, u32[]{:S(2)}, u32[]{:S(2)}) collective-permute-start(bf16[1024,256]{1,0:T(8,128)(2,1)} %get-tuple-element.213), channel_id=1, source_target_pairs={{0,16},{4,20},{8,24},{12,28},{16,32},{20,36},{24,40},{28,44},{32,4... | collective-permute-start | bytes 1572872 | tf_op jit(solution)/shard_map/while/body/eval_jaxpr/ppermute | solution.py:11
  580.1 17.6 %collective-permute-start.1 = (bf16[1024,256]{1,0:T(8,128)(2,1)}, bf16[1024,256]{1,0:T(8,128)(2,1)S(1)}, u32[]{:S(2)}, u32[]{:S(2)}) collective-permute-start(bf16[1024,256]{1,0:T(8,128)(2,1)} %get-tuple-element.213), channel_id=1, source_target_pairs={{0,16},{4,20},{8,24},{12,28},{16,32},{20,36},{24,40},{28,44},{32,4... | collective-permute-start | bytes 1572872 | tf_op jit(solution)/shard_map/while/body/eval_jaxpr/ppermute | solution.py:11
  599.3 16.7 %collective-permute-start.1 = (bf16[1024,256]{1,0:T(8,128)(2,1)}, bf16[1024,256]{1,0:T(8,128)(2,1)S(1)}, u32[]{:S(2)}, u32[]{:S(2)}) collective-permute-start(bf16[1024,256]{1,0:T(8,128)(2,1)} %get-tuple-element.213), channel_id=1, source_target_pairs={{0,16},{4,20},{8,24},{12,28},{16,32},{20,36},{24,40},{28,44},{32,4... | collective-permute-start | bytes 1572872 | tf_op jit(solution)/shard_map/while/body/eval_jaxpr/ppermute | solution.py:11
  656.0 682.5 %all-reduce.8.cloned.1.call-start = ((), (), s32[]{:S(2)}) async-start(), calls=%async_computation.1 | async-start | bytes 393216 | tf_op jit(solution)/shard_map/psum | solution.py:91
  (15 other events, 499.7 us)
Sparse Core Ops, SparseCore 0:
  656.1 41.5 all-reduce.5
  702.4 636.0 all-reduce.7
where the time goes:
time: 1350 us
  waiting for transfers between devices  1200 us (89%)
  local copies, waits for them, and re-layouts  76.9 us (6%)
  blocking collectives  25.9 us (2%)
  matrix products  21.3 us (2%)
  between operations  14.8 us (1%)
    psum x1, waiting for transfers between devices, local(): grad_weight = lax.psum(partial_weight, 'blk')  634 us
    ppermute x34, waiting for transfers between devices, shifted(): lax.ppermute(value, axis, [(i, (i + by) % length) for i in range(length)])  523 us
    psum x1, waiting for transfers between devices, local(): second = lax.psum(propagate(first), 'rep')  40.3 us
  transfers between devices with their start and end apart: 36, of which 36 were waited for; matrix products, arithmetic and copies ran while one was open for 1% of the time, Pallas kernels for 0%

commit v1 on v0

v1 whole, which is shorter than its diff:
```python
import functools
import math

import jax
import jax.numpy as jnp
from jax import lax
from jax.experimental import pallas as pl
from jax.experimental.pallas import tpu as pltpu
from jax.sharding import PartitionSpec as P

MESH = pl.DeviceIdType.MESH
T = 256
WIDE = 192
RELAY = 64


def xor(a, b):
    return a + b - 2 * a * b


def kernel(
    rows_ref, cols_ref, offs_ref, heat_ref, cot_ref, feat_ref, weight_ref, tiles_hbm,
    gw_ref, gf_ref,
    field0, field1, tiles, own, acc, core_in, chip_out, chip_in, qsum, comb, gwp, g1, s1, g2, s2, gfin,
    tile_sem, own_sem, relay_sem, gy_sem, g0_sem, grest_sem, r1_sem, send_sem, self_sem,
    ex_send, ex_recv, cb_send, cb_recv, gw_send, gw_recv,
):
    blk = lax.axis_index("blk")
    rep = lax.axis_index("rep")
    z = blk // 8
    y = (blk // 2) % 4
    xh = blk % 2
    xl = rep // 2
    c = rep % 2
    n = xor(c, xh)
    hx = xor(xl, xh)
    own_tile = hx * 2 + c

    def dev(xh_, xl_, y_, z_, c_):
        return (z_ * 8 + y_ * 2 + xh_, xl_ * 2 + c_)

    def delta2(xh_, xl_):
        return (1 - xh_) * (3 - xl_) + xh_ * xl_

    relay_one = dev(xh, xl, (y + 1 - xl) % 4, z, 0)
    relay_two = dev(1 - xh, xl, (y + delta2(xh, xl)) % 4, z, 1)
    one_is_self = xl * (1 - c)

    yr = ((1 - c) * (y - 1 + xl) + c * (y - delta2(1 - xh, xl)) + 4) % 4
    hr = xor(xl, n)
    src_xh = xor(xh, c)
    ey = 2 * hx - 1
    yc = ((1 - c) * (y - ey - 1 + xl) + c * (y - ey - delta2(1 - xh, xl)) + 8) % 4

    z_up = dev(xh, xl, y, (z + 1) % 8, c)
    z_dn = dev(xh, xl, y, (z + 7) % 8, c)
    y_chain = dev(xh, xl, (y + ey + 4) % 4, z, c)
    y_other = dev(xh, xl, (y - ey + 4) % 4, z, c)
    x_near = dev(xh, 1 - xl, y, z, c)
    x_far = dev(1 - xh, 1 - xl, y, z, 1 - c)
    sibling = dev(xh, xl, y, z, 1 - c)

    barrier = pltpu.get_barrier_semaphore()

    def greet(device):
        pl.semaphore_signal(barrier, inc=1, device_id=device, device_id_type=MESH)

    src_y = yr
    src_first = dev(src_xh, xl, src_y, z, 0)
    src_second = dev(src_xh, xl, src_y, z, 1)

    @pl.when(one_is_self == 0)
    def _():
        greet(src_first)

    greet(src_second)
    for device in (y_chain, y_other, x_near, x_far, sibling):
        greet(device)
    for step in range(1, 8):
        greet(dev(xh, xl, y, (z + step) % 8, c))
    for step in range(1, 8):
        place = (y * 2 + xh + step) % 8
        greet(dev(place % 2, xl, place // 2, z, c))
    pl.semaphore_wait(barrier, 21 - one_is_self)

    pltpu.make_async_copy(tiles_hbm, tiles, tile_sem).start()
    own[0] = cot_ref[pl.ds(pl.multiple_of(own_tile * T, T), T), :]

    def send(src, dst, ssem, rsem, device):
        pltpu.make_async_remote_copy(
            src_ref=src, dst_ref=dst, send_sem=ssem, recv_sem=rsem, device_id=device, device_id_type=MESH
        ).start()

    def drain(ref, sem):
        pltpu.make_async_copy(ref, ref, sem).wait()

    wide = pl.ds(0, WIDE)
    thin = pl.ds(WIDE, T - WIDE)

    def propagate(p, buf):

        def zp(i):
            return (z + (0, 7, 6, 5, 1, 2, 3, 4)[i]) % 8

        def relay(i):
            return buf.at[pl.ds(RELAY + zp(i) * 2, 2)]

        def spot(i, ysrc, half):
            return (zp(i) * 2 + ysrc // 2) * 4 + half * 2

        mine = own.at[p]
        slot = RELAY + z * 2 + c

        @pl.when(one_is_self == 1)
        def _():
            pltpu.make_async_copy(mine, buf.at[slot], relay_sem.at[p, 0]).start()

        @pl.when(one_is_self == 0)
        def _():
            send(mine, buf.at[slot], self_sem.at[p], relay_sem.at[p, 0], relay_one)

        send(mine, buf.at[slot], send_sem.at[p, 0], relay_sem.at[p, 0], relay_two)

        def along_z(i, up, index):
            tiles_of = pl.ds(RELAY + zp(i) * 2, 2)
            if index == 7 and up:
                tiles_of = pl.ds(RELAY + zp(i) * 2, 1)
            elif index == 7:
                tiles_of = pl.ds(RELAY + zp(i) * 2 + 1, 1)
            sem = relay_sem.at[p, 8 if index == 7 and not up else index]
            part = buf.at[tiles_of, wide]
            send(part, part, send_sem.at[p, 1], sem, z_up if up else z_dn)

        def over_plane(i):
            rows = pl.ds(0, T) if i == 0 else wide
            ssem = send_sem.at[p, 2 if i == 0 else 3]
            rest = g0_sem.at[p] if i == 0 else grest_sem.at[p]
            src = buf.at[pl.ds(RELAY + zp(i) * 2, 2), rows]
            dst = buf.at[pl.ds(spot(i, yr, hr), 2), rows]
            send(src, dst, ssem, gy_sem.at[p, i], y_chain)
            send(src, dst, ssem, rest, y_other)
            send(src, dst, ssem, rest, x_near)

        def far(i):
            rows = pl.ds(0, T) if i == 0 else wide
            ssem = send_sem.at[p, 2 if i == 0 else 3]
            rest = g0_sem.at[p] if i == 0 else grest_sem.at[p]
            drain(buf.at[pl.ds(0, 2), rows], gy_sem.at[p, i])
            chained = spot(i, yc, hr)
            src = (1 - n) * (RELAY + zp(i) * 2) + n * chained
            dst = (1 - n) * spot(i, yr, hr) + n * chained
            send(buf.at[pl.ds(src, 2), rows], buf.at[pl.ds(dst, 2), rows], ssem, rest, x_far)

        def thin_z(i, up, index):
            first, count = zp(i) * 8, 8
            if index == 7:
                count = 4
                if not up:
                    first = first + 4
            part = buf.at[pl.ds(first, count), thin]
            sem = r1_sem.at[p, 8 if index == 7 and not up else index]
            send(part, part, send_sem.at[p, 4], sem, z_up if up else z_dn)

        drain(buf.at[pl.ds(0, 2)], relay_sem.at[p, 0])
        along_z(0, True, 1)
        along_z(0, False, 4)
        over_plane(0)
        after_up = {1: 2, 2: 3, 3: 7}
        after_dn = {4: 5, 5: 6, 6: 7}

        def relay_step(s):
            for i, up, follow in ((s, True, after_up[s]), (s + 3, False, after_dn[s + 3])):
                drain(buf.at[pl.ds(0, 2), wide], relay_sem.at[p, i])
                along_z(i, up, follow)
                over_plane(i)

        def thin_step(s):
            for i, up, follow in ((s, True, after_up[s]), (s + 3, False, after_dn[s + 3])):
                drain(buf.at[pl.ds(0, 8), thin], r1_sem.at[p, i])
                thin_z(i, up, follow)

        relay_step(1)
        far(0)
        drain(buf.at[pl.ds(0, 6)], g0_sem.at[p])
        thin_z(0, True, 1)
        thin_z(0, False, 4)
        relay_step(2)
        far(1)
        far(4)
        thin_step(1)
        relay_step(3)
        far(2)
        far(5)
        thin_step(2)
        drain(buf.at[pl.ds(0, 1), wide], relay_sem.at[p, 7])
        drain(buf.at[pl.ds(0, 1), wide], relay_sem.at[p, 8])
        over_plane(7)
        far(3)
        far(6)
        thin_step(3)
        far(7)

        if p == 0:
            drain(tiles, tile_sem)

        acc[...] = jnp.zeros_like(acc)

        drain(buf.at[pl.ds(0, 42), wide], grest_sem.at[p])
        drain(buf.at[pl.ds(0, 4), thin], r1_sem.at[p, 7])
        drain(buf.at[pl.ds(0, 4), thin], r1_sem.at[p, 8])

        live = offs_ref[16]

        def slot_step(k, carry_):
            row = rows_ref[k]
            col = cols_ref[k] % 4
            tile = buf[((row // 16) % 16) * 4 + row % 4]
            term = lax.dot_general(
                tiles[k], tile, (((0,), (0,)), ((), ())), preferred_element_type=jnp.float32
            )
            for t in range(4):
                hit = jnp.logical_and(col == t, k < live)
                acc[t] += jnp.where(hit, term, 0.0)
            return carry_

        lax.fori_loop(0, 16, slot_step, 0)

        for g in range(2):
            send(acc.at[g * 2 + 1 - c], core_in.at[p, g], ex_send.at[p, 0], ex_recv.at[p, 0], sibling)
        drain(core_in.at[p], ex_recv.at[p, 0])
        give = (1 - hx) * 2 + c
        chip_out[p] = (acc[give] + core_in[p, 1 - hx]).astype(jnp.bfloat16)
        send(chip_out.at[p], chip_in.at[p], ex_send.at[p, 1], ex_recv.at[p, 1], x_near)
        drain(chip_in.at[p], ex_recv.at[p, 1])
        qsum[...] = acc[own_tile] + core_in[p, hx] + chip_in[p].astype(jnp.float32)
        own[p + 1] = qsum[...].astype(jnp.bfloat16)

        @pl.when(one_is_self == 0)
        def _():
            drain(mine, self_sem.at[p])

        drain(mine, send_sem.at[p, 0])
        drain(buf.at[pl.ds(0, 14), wide], send_sem.at[p, 1])
        drain(buf.at[pl.ds(0, 8)], send_sem.at[p, 2])
        drain(buf.at[pl.ds(0, 56), wide], send_sem.at[p, 3])
        drain(buf.at[pl.ds(0, 56), thin], send_sem.at[p, 4])
        drain(core_in.at[p], ex_send.at[p, 0])
        drain(chip_in.at[p], ex_send.at[p, 1])

    propagate(0, field0)
    propagate(1, field1)

    tv = jnp.full((1, T), heat_ref[0], jnp.float32)
    total = 1.0 + tv + tv * tv / 2.0
    combined = (
        (1.0 / total) * own[0].astype(jnp.float32)
        + (tv / total) * own[1].astype(jnp.float32)
        + ((tv * tv / 2.0) / total) * qsum[...]
    ).astype(jnp.bfloat16)
    comb[own_tile] = combined
    other_tile = (1 - hx) * 2 + c
    send(comb.at[own_tile], comb.at[own_tile], cb_send.at[0], cb_recv.at[0], x_near)
    send(comb.at[own_tile], comb.at[own_tile], cb_send.at[1], cb_recv.at[1], sibling)
    drain(comb.at[0], cb_recv.at[0])
    send(comb.at[other_tile], comb.at[other_tile], cb_send.at[2], cb_recv.at[2], sibling)
    drain(comb.at[0], cb_recv.at[1])
    drain(comb.at[0], cb_recv.at[2])

    partial = jnp.zeros((192, T), jnp.float32)
    for t in range(4):
        partial += lax.dot_general(
            feat_ref[pl.ds(t * T, T), :], comb[t], (((0,), (0,)), ((), ())), preferred_element_type=jnp.float32
        )
    gwp[...] = partial * (1.0 / 256.0)

    piece = 24
    my_rows = pl.ds(pl.multiple_of(z * piece, 8), piece)
    for step in range(1, 8):
        zt = (z + step) % 8
        send(
            gwp.at[pl.ds(pl.multiple_of(zt * piece, 8), piece)], g1.at[z],
            gw_send.at[0], gw_recv.at[0], dev(xh, xl, y, zt, c),
        )
    g1[z] = gwp[my_rows, :]

    for t in range(4):
        gf_ref[pl.ds(t * T, T), :] = lax.dot_general(
            comb[t], weight_ref[...], (((1,), (1,)), ((), ())), preferred_element_type=jnp.float32
        ).astype(jnp.bfloat16)

    drain(g1.at[pl.ds(0, 7)], gw_recv.at[0])
    s1[...] = functools.reduce(lambda a, b: a + b, [g1[i] for i in range(8)])
    here = y * 2 + xh
    for step in range(1, 8):
        place = (here + step) % 8
        send(s1, g2.at[here], gw_send.at[1], gw_recv.at[1], dev(place % 2, xl, place // 2, z, c))
    g2[here] = s1[...]
    drain(g2.at[pl.ds(0, 7)], gw_recv.at[1])
    s2[...] = functools.reduce(lambda a, b: a + b, [g2[i] for i in range(8)])
    for step in range(1, 8):
        send(s2, gfin.at[z], gw_send.at[2], gw_recv.at[2], dev(xh, xl, y, (z + step) % 8, c))
    gfin[z] = s2[...]
    drain(gfin.at[pl.ds(0, 7)], gw_recv.at[2])
    for i in range(8):
        gw_ref[pl.ds(i * piece, piece), :] = gfin[i]

    for i in range(3):
        drain(comb.at[0], cb_send.at[i])
        drain(g1.at[pl.ds(0, 7)], gw_send.at[i])


def local(cotangent, features, weight, heat_time, tile_values, tile_row, tile_col, section_offsets):
    vmem = pl.BlockSpec(memory_space=pltpu.VMEM)
    smem = pl.BlockSpec(memory_space=pltpu.SMEM)
    f32, bf16 = jnp.float32, jnp.bfloat16
    dma = pltpu.SemaphoreType.DMA
    return pl.pallas_call(
        kernel,
        out_shape=(
            jax.ShapeDtypeStruct((192, T), f32),
            jax.ShapeDtypeStruct((1024, 192), bf16),
        ),
        in_specs=[smem, smem, smem, smem, vmem, vmem, vmem, pl.BlockSpec(memory_space=pl.ANY)],
        out_specs=(vmem, vmem),
        scratch_shapes=[
            pltpu.VMEM((RELAY + 16, T, T), bf16),
            pltpu.VMEM((RELAY + 16, T, T), bf16),
            pltpu.VMEM((16, T, T), bf16),
            pltpu.VMEM((3, T, T), bf16),
            pltpu.VMEM((4, T, T), f32),
            pltpu.VMEM((2, 2, T, T), f32),
            pltpu.VMEM((2, T, T), bf16),
            pltpu.VMEM((2, T, T), bf16),
            pltpu.VMEM((T, T), f32),
            pltpu.VMEM((4, T, T), bf16),
            pltpu.VMEM((192, T), f32),
            pltpu.VMEM((8, 24, T), f32),
            pltpu.VMEM((24, T), f32),
            pltpu.VMEM((8, 24, T), f32),
            pltpu.VMEM((24, T), f32),
            pltpu.VMEM((8, 24, T), f32),
            dma, dma,
            dma((2, 9)),
            dma((2, 8)),
            dma((2,)),
            dma((2,)),
            dma((2, 9)),
            dma((2, 5)),
            dma((2,)),
            dma((2, 2)), dma((2, 2)),
            dma((3,)), dma((3,)),
            dma((3,)), dma((3,)),
        ],
        compiler_params=pltpu.CompilerParams(
            collective_id=0, has_side_effects=True, vmem_limit_bytes=48 << 20
        ),
        cost_estimate=pl.CostEstimate(flops=1_300_000_000, bytes_accessed=4_000_000, transcendentals=0),
        name="diffuse",
    )(tile_row, tile_col, section_offsets, heat_time, cotangent, features, weight, tile_values)


def solution(mesh):
    in_specs = (
        P("blk", None),
        P("blk", "rep"),
        P("rep", None),
        P(),
        P(("blk", "rep"), None, None),
        P(("blk", "rep")),
        P(("blk", "rep")),
        P(("blk", "rep")),
    )
    out_specs = (P("rep", None), P("blk", "rep"))
    return jax.shard_map(local, mesh=mesh, in_specs=in_specs, out_specs=out_specs, check_vma=False)
```

time: 1350 us -> 176 us (0.13)
  waiting for transfers between devices: 1200 us -> 0 us
  Pallas kernels: 0 us -> 165 us
  local copies, waits for them, and re-layouts: 76.9 us -> 8.3 us
  blocking collectives: 25.9 us -> 0 us
  matrix products: 21.3 us -> 0 us
  between operations: 14.8 us -> 1.3 us
    psum x2 -> x0, waiting for transfers between devices: 675 us -> none  [the longest x1 634 us: local(): grad_weight = lax.psum(partial_weight, 'blk')]
    ppermute x34 -> x0, waiting for transfers between devices: 523 us -> none  [shifted(): lax.ppermute(value, axis, [(i, (i + by) % length) for i in range(length)])]
    pallas_call x0 -> x1, Pallas kernels: none -> 165 us  [local(): pl.pallas_call(kernel, out_shape=(jax.ShapeDtypeStruct((192, T), f32), ja...]
    dynamic_update_slice x32 -> x0, local copies, waits for them, and re-layouts: 33.2 us -> none  [the longest x30 25.1 us: advance(): lax.dynamic_update_index_in_dim(holder, source_block, section_idx, 0)]
    psum x1 -> x0, blocking collectives: 25.9 us -> none  [local(): first = lax.psum(partial_first, 'rep').astype(jnp.bfloat16)]
    dot_general x6 -> x0, matrix products: 21.3 us -> none  [the longest x2 9.58 us: absorb(): jnp.dot(target_table, terms.reshape(slot_count, tile_size * width), preci...]
  transfers between devices with their start and end apart: 36 -> 0, of which waited for: 36 -> 0; matrix products, arithmetic and copies ran while one was open for 1% -> 0% of each run, Pallas kernels for 0% -> 0%
where the time goes in v1:
time: 176 us; the launch traced here: 175 us
  Pallas kernels  165 us (94%)
  local copies, waits for them, and re-layouts  8.3 us (5%)
    pallas_call x1, Pallas kernels, local(): pl.pallas_call(kernel, out_shape=(jax.ShapeDtypeStruct((192, T), f32), ja...  165 us
    unnamed x14, local copies, waits for them, and re-layouts  7.36 us

profile of v1, /device:TPU:2, one launch (start us, length us, event | category | flops | bytes accessed | tf_op | source)
XLA Modules:
  0.0 174.7 jit_solution(1105314819976711921)
XLA Ops:
  1.3 1.2 copy.10.feat_ref
  2.5 0.0 copy-start
  2.5 1.6 copy-done
  4.1 0.0 copy-start.1
  4.1 1.0 copy-done.1
  5.1 0.0 copy-start.2
  5.1 0.9 copy-done.2
  6.0 0.0 copy-start.3
  6.0 0.7 copy-done.3
  6.7 0.0 copy-start.4
  6.7 0.7 copy-done.4
  7.3 0.0 copy-start.5
  7.3 0.7 copy-done.5
  8.0 165.1 %diffuse.1 = (f32[192,256]{1,0:T(8,128)S(1)}, bf16[1024,192]{1,0:T(8,128)(2,1)S(1)}) custom-call(s32[16]{0:T(128)S(1)} %copy-done.3, s32[16]{0:T(128)S(1)} %copy-done.4, s32[17]{0:T(128)S(1)} %copy-done.5, f32[1]{0:T(128)S(6)} %copy.13.heat_ref, bf16[1024,256]{1,0:T(8,128)(2,1)S(1)} %copy-done.1, bf16[1024,192]{1,0:T(8,128)(2,1)S(1)} %copy.10.feat_ref, ...), custom_call_target="tpu_custom_call" | custom-call | flops 1300000000 | bytes 4000000 | tf_op jit(solution)/shard_map/diffuse/pallas_call | solution.py:317
  173.1 0.9 copy.11
  174.0 0.7 copy.14
Async XLA Ops:
  2.5 1.6 copy-start
  4.1 1.0 copy-start.1
  5.1 0.9 copy-start.2
  6.0 0.7 copy-start.3
  6.7 0.7 copy-start.4
  7.3 0.7 copy-start.5

commit v2 on v0

v2 whole, which is shorter than its diff:
```python
import functools

import jax
import jax.numpy as jnp
from jax import lax
from jax.experimental import pallas as pl
from jax.experimental.pallas import tpu as pltpu
from jax.sharding import PartitionSpec as P

MESH = pl.DeviceIdType.MESH
T = 256
THIN = 64
CHUNK = 64
RELAY = 64
PIECE = 24


def xor(a, b):
    return a + b - 2 * a * b


def kernel(
    rows_hbm, cols_hbm, offs_hbm, heat_ref, cot_hbm, feat_hbm, weight_hbm, tiles_hbm,
    gw_ref, gf_ref,
    rows_ref, cols_ref, offs_ref, cot, feat, weight, tiles,
    field0, field1, own, acc, core_in, chip_out, chip_in, pair_out, pair_in, comb,
    gwp, g1, s1, g2, s2, gfin,
    load_sem, small_sem, cot_sem,
    rt_sem, relay_sem, gyt_sem, gy_sem, g0_sem, grest_sem, ring_sem, send_sem, self_sem,
    ex_send, ex_recv, chip_send, chip_recv, pair_send, pair_recv, cb_send, cb_recv, gw_send, gw_recv,
):
    blk = lax.axis_index("blk")
    rep = lax.axis_index("rep")
    z = blk // 8
    y = (blk // 2) % 4
    xh = blk % 2
    xl = rep // 2
    c = rep % 2
    n = xor(c, xh)
    hx = xor(xl, xh)
    own_tile = hx * 2 + c
    other_tile = (1 - hx) * 2 + c

    def dev(xh_, xl_, y_, z_, c_):
        return (z_ * 8 + y_ * 2 + xh_, xl_ * 2 + c_)

    def delta2(xh_, xl_):
        return (1 - xh_) * (3 - xl_) + xh_ * xl_

    relay_one = dev(xh, xl, (y + 1 - xl) % 4, z, 0)
    relay_two = dev(1 - xh, xl, (y + delta2(xh, xl)) % 4, z, 1)
    relay_two_near = dev(1 - xh, 1 - xl, (y + delta2(xh, 1 - xl)) % 4, z, 1)
    one_is_self = xl * (1 - c)

    yr = ((1 - c) * (y - 1 + xl) + c * (y - delta2(1 - xh, xl)) + 4) % 4
    hr = xor(xl, n)
    ey = 2 * hx - 1
    yc = ((1 - c) * (y - ey - 1 + xl) + c * (y - ey - delta2(1 - xh, xl)) + 8) % 4

    z_up = dev(xh, xl, y, (z + 1) % 8, c)
    z_dn = dev(xh, xl, y, (z + 7) % 8, c)
    y_chain = dev(xh, xl, (y + ey + 4) % 4, z, c)
    y_other = dev(xh, xl, (y - ey + 4) % 4, z, c)
    x_near = dev(xh, 1 - xl, y, z, c)
    x_far = dev(1 - xh, 1 - xl, y, z, 1 - c)
    sibling = dev(xh, xl, y, z, 1 - c)
    here = y * 2 + xh

    def plane_peer(step):
        place = (here + step) % 8
        return place, dev(place % 2, xl, place // 2, z, c)

    def z_peer(step):
        zt = (z + step) % 8
        return zt, dev(xh, xl, y, zt, c)

    def load(src, dst, sem):
        pltpu.make_async_copy(src, dst, sem).start()

    for i, tile in enumerate((own_tile, other_tile)):
        load(cot_hbm.at[pl.ds(pl.multiple_of(tile * T, T), T)], cot.at[i], cot_sem.at[i])
    load(rows_hbm, rows_ref, small_sem.at[0])
    load(cols_hbm, cols_ref, small_sem.at[1])
    load(offs_hbm, offs_ref, small_sem.at[2])
    load(tiles_hbm, tiles, load_sem.at[0])
    load(feat_hbm, feat, load_sem.at[1])
    load(weight_hbm, weight, load_sem.at[2])

    barrier = pltpu.get_barrier_semaphore()

    def greet(device):
        pl.semaphore_signal(barrier, inc=1, device_id=device, device_id_type=MESH)

    @pl.when(c == 0)
    def _():
        @pl.when(one_is_self == 0)
        def _():
            greet(dev(xh, xl, yr, z, 0))

        greet(dev(xh, xl, yr, z, 1))

    @pl.when(c == 1)
    def _():
        for core in range(2):
            greet(dev(1 - xh, xl, yr, z, core))
            greet(dev(1 - xh, 1 - xl, yr, z, core))

    for device in (y_chain, y_other, x_near, x_far, sibling):
        greet(device)
    for step in range(1, 8):
        greet(z_peer(step)[1])
        greet(plane_peer(step)[1])

    def send(src, dst, ssem, rsem, device):
        pltpu.make_async_remote_copy(
            src_ref=src, dst_ref=dst, send_sem=ssem, recv_sem=rsem, device_id=device, device_id_type=MESH
        ).start()

    def drain(ref, sem):
        pltpu.make_async_copy(ref, ref, sem).wait()

    def turned(ref):
        return ref[...].astype(jnp.float32).T.astype(jnp.bfloat16)

    drain(cot.at[0], cot_sem.at[0])
    own[0] = turned(cot.at[0])
    drain(cot.at[1], cot_sem.at[1])
    own[2] = turned(cot.at[1])

    pl.semaphore_wait(barrier, 22 - one_is_self)

    thin = pl.ds(0, THIN)
    wide = pl.ds(THIN, T - THIN)
    follow_of = {1: 2, 2: 3, 3: 7, 4: 5, 5: 6, 6: 7}

    def zp(i):
        return (z + (0, 7, 6, 5, 1, 2, 3, 4)[i]) % 8

    def spot(i, ysrc):
        return (zp(i) * 2 + ysrc // 2) * 4 + hr * 2

    def hand_out(p, buf, rows, to_two, two):
        mine = own.at[p, rows]
        slot = RELAY + z * 2 + c
        sem = rt_sem.at[p] if rows is thin else relay_sem.at[p, 0, c]

        @pl.when(one_is_self == 1)
        def _():
            load(mine, buf.at[slot, rows], sem)

        @pl.when(one_is_self == 0)
        def _():
            send(mine, buf.at[slot, rows], self_sem.at[p], sem, relay_one)

        send(two.at[rows], buf.at[slot, rows], send_sem.at[p, 0], sem, to_two)

    def gather(p, buf):
        def over_plane(i, tile, count, rows, ssem, chain_sem, rest):
            src = buf.at[pl.ds(RELAY + zp(i) * 2 + tile, count), rows]
            dst = buf.at[pl.ds(spot(i, yr) + tile, count), rows]
            send(src, dst, ssem, chain_sem, y_chain)
            send(src, dst, ssem, rest, y_other)
            send(src, dst, ssem, rest, x_near)

        def far(i, tile, count, rows, ssem, chain_sem, rest):
            drain(buf.at[pl.ds(0, count), rows], chain_sem)
            chained = spot(i, yc) + tile
            src = (1 - n) * (RELAY + zp(i) * 2 + tile) + n * chained
            dst = (1 - n) * (spot(i, yr) + tile) + n * chained
            send(buf.at[pl.ds(src, count), rows], buf.at[pl.ds(dst, count), rows], ssem, rest, x_far)

        def along_z(i, tile, up, follow):
            part = buf.at[RELAY + zp(i) * 2 + tile, wide]
            send(part, part, send_sem.at[p, 1], relay_sem.at[p, follow, tile], z_up if up else z_dn)

        def ring(i, block, up, follow):
            part = buf.at[pl.ds(zp(i) * 8 + block * 4, 4), thin]
            send(part, part, send_sem.at[p, 4], ring_sem.at[p, follow, block], z_up if up else z_dn)

        def wide_plane(i, tile):
            over_plane(i, tile, 1, wide, send_sem.at[p, 3], gy_sem.at[p, i, tile], grest_sem.at[p])

        def wide_far(i):
            for tile in range(2):
                far(i, tile, 1, wide, send_sem.at[p, 3], gy_sem.at[p, i, tile], grest_sem.at[p])

        def wide_wait(i, tile):
            drain(buf.at[0, wide], relay_sem.at[p, i, tile])

        def wide_step(s):
            for tile in range(2):
                for i, up in ((s, True), (s + 3, False)):
                    wide_wait(i, tile)
                    if s < 3 or tile == 1 - up:
                        along_z(i, tile, up, follow_of[i])
                    wide_plane(i, tile)

        def thin_step(s):
            for block in range(2):
                for i, up in ((s, True), (s + 3, False)):
                    drain(buf.at[pl.ds(0, 4), thin], ring_sem.at[p, i, block])
                    if s < 3 or block == 1 - up:
                        ring(i, block, up, follow_of[i])

        drain(buf.at[pl.ds(0, 2), thin], rt_sem.at[p])
        over_plane(0, 0, 2, thin, send_sem.at[p, 2], gyt_sem.at[p], g0_sem.at[p])
        for tile in range(2):
            wide_wait(0, tile)
            along_z(0, tile, True, 1)
            along_z(0, tile, False, 4)
            wide_plane(0, tile)
        far(0, 0, 2, thin, send_sem.at[p, 2], gyt_sem.at[p], g0_sem.at[p])
        drain(buf.at[pl.ds(0, 6), thin], g0_sem.at[p])
        for block in range(2):
            ring(0, block, True, 1)
            ring(0, block, False, 4)
        wide_step(1)
        wide_far(0)
        thin_step(1)
        wide_step(2)
        wide_far(1)
        wide_far(4)
        thin_step(2)
        wide_step(3)
        wide_far(2)
        wide_far(5)
        thin_step(3)
        for tile in range(2):
            wide_wait(7, tile)
            wide_plane(7, tile)
        wide_far(3)
        wide_far(6)
        wide_far(7)
        drain(buf.at[pl.ds(0, 48), wide], grest_sem.at[p])
        for block in range(2):
            drain(buf.at[pl.ds(0, 4), thin], ring_sem.at[p, 7, block])

    def part(j):
        return pl.ds(j * CHUNK, CHUNK)

    parts = T // CHUNK

    def products(buf, j):
        rows = part(j)
        total = jnp.zeros((4 * CHUNK, T), jnp.float32)
        for k in range(16):
            row = rows_ref[k]
            col = cols_ref[k] % 4
            alive = k < offs_ref[16]
            tile = buf[((row // 16) % 16) * 4 + row % 4, rows, :]
            picked = [
                jnp.where(jnp.logical_and(col == t, alive), tile, jnp.zeros_like(tile)) for t in range(4)
            ]
            total = total + jnp.dot(
                jnp.concatenate(picked, axis=0), tiles[k], preferred_element_type=jnp.float32
            )
        for t in range(4):
            acc[t, rows, :] = total[t * CHUNK : (t + 1) * CHUNK]

    def swap_cores(p, j):
        rows = part(j)
        for g in range(2):
            send(
                acc.at[g * 2 + 1 - c, rows], core_in.at[p, g, rows],
                ex_send.at[p, j], ex_recv.at[p, j], sibling,
            )

    def await_cores(p, j):
        drain(core_in.at[p, pl.ds(0, 2), part(j)], ex_recv.at[p, j])

    hand_out(0, field0, thin, relay_two_near, own.at[2])
    hand_out(0, field0, wide, relay_two_near, own.at[2])
    gather(0, field0)
    for i, ref in enumerate((rows_ref, cols_ref, offs_ref)):
        drain(ref, small_sem.at[i])
    drain(tiles, load_sem.at[0])

    def pass_on(j):
        rows = part(j)
        await_cores(0, j)
        chip_out[rows, :] = (acc[other_tile, rows, :] + core_in[0, 1 - hx, rows, :]).astype(jnp.bfloat16)
        send(chip_out.at[rows], chip_in.at[rows], chip_send.at[j], chip_recv.at[j], x_near)

    def close_first(j):
        rows = part(j)
        drain(chip_in.at[rows], chip_recv.at[j])
        own[1, rows, :] = (
            acc[own_tile, rows, :] + core_in[0, hx, rows, :] + chip_in[rows, :].astype(jnp.float32)
        ).astype(jnp.bfloat16)

    for j in range(parts):
        products(field0, j)
        swap_cores(0, j)
        if j >= 1:
            pass_on(j - 1)
        if j >= 2:
            close_first(j - 2)
        if j == 2:
            hand_out(1, field1, thin, relay_two, own.at[1])
    pass_on(parts - 1)
    close_first(parts - 2)
    close_first(parts - 1)

    hand_out(1, field1, wide, relay_two, own.at[1])
    gather(1, field1)
    for j in range(parts):
        drain(core_in.at[0, pl.ds(0, 2), part(j)], ex_send.at[0, j])

    tv = jnp.full((1, T), heat_ref[0], jnp.float32)
    total = 1.0 + tv + tv * tv / 2.0
    coef0 = 1.0 / total
    coef1 = tv / total
    coef2 = (tv * tv / 2.0) / total

    def pair_up(j):
        rows = part(j)
        await_cores(1, j)
        mine = coef2 * (acc[own_tile, rows, :] + core_in[1, hx, rows, :])
        mine += coef0 * own[0, rows, :].astype(jnp.float32) + coef1 * own[1, rows, :].astype(jnp.float32)
        acc[own_tile, rows, :] = mine
        pair_out[0, rows, :] = mine.astype(jnp.bfloat16)
        theirs = coef2 * (acc[other_tile, rows, :] + core_in[1, 1 - hx, rows, :])
        acc[other_tile, rows, :] = theirs
        pair_out[1, rows, :] = theirs.astype(jnp.bfloat16)
        for i in range(2):
            send(pair_out.at[i, rows], pair_in.at[1 - i, rows], pair_send.at[j], pair_recv.at[j], x_near)

    def close_second(j):
        rows = part(j)
        drain(pair_in.at[pl.ds(0, 2), rows], pair_recv.at[j])
        for i, tile in enumerate((own_tile, other_tile)):
            comb[tile, rows, :] = (acc[tile, rows, :] + pair_in[i, rows, :].astype(jnp.float32)).astype(
                jnp.bfloat16
            )
            send(comb.at[tile, rows], comb.at[tile, rows], cb_send, cb_recv, sibling)

    for j in range(parts):
        products(field1, j)
        swap_cores(1, j)
        if j >= 1:
            pair_up(j - 1)
        if j >= 2:
            close_second(j - 2)
    pair_up(parts - 1)
    close_second(parts - 2)
    close_second(parts - 1)
    drain(feat, load_sem.at[1])
    drain(weight, load_sem.at[2])
    drain(comb.at[pl.ds(0, 2)], cb_recv)

    partial = jnp.zeros((192, T), jnp.float32)
    for t in range(4):
        partial += lax.dot_general(
            feat[:, t * T : (t + 1) * T], comb[t], (((1,), (1,)), ((), ())),
            preferred_element_type=jnp.float32,
        )
    gwp[...] = partial * (1.0 / 256.0)

    for step in range(1, 8):
        place, device = plane_peer(step)
        rows = pl.ds(pl.multiple_of(place * PIECE, 8), PIECE)
        send(gwp.at[rows], g1.at[here], gw_send.at[0], gw_recv.at[0], device)
    g1[here] = gwp[pl.ds(pl.multiple_of(here * PIECE, 8), PIECE), :]

    for t in range(4):
        gf_ref[:, t * T : (t + 1) * T] = jnp.dot(
            weight[...], comb[t], preferred_element_type=jnp.float32
        ).astype(jnp.bfloat16)

    drain(g1.at[pl.ds(0, 7)], gw_recv.at[0])
    s1[...] = functools.reduce(lambda a, b: a + b, [g1[i] for i in range(8)])
    for step in range(1, 8):
        send(s1, g2.at[z], gw_send.at[1], gw_recv.at[1], z_peer(step)[1])
    g2[z] = s1[...]
    drain(g2.at[pl.ds(0, 7)], gw_recv.at[1])
    s2[...] = functools.reduce(lambda a, b: a + b, [g2[i] for i in range(8)])
    for step in range(1, 8):
        send(s2, gfin.at[here], gw_send.at[2], gw_recv.at[2], plane_peer(step)[1])
    gfin[here] = s2[...]

    for p, buf in enumerate((field0, field1)):
        @pl.when(one_is_self == 0)
        def _(p=p):
            drain(own.at[p], self_sem.at[p])

        drain(own.at[p], send_sem.at[p, 0])
        drain(buf.at[pl.ds(0, 14), wide], send_sem.at[p, 1])
        drain(buf.at[pl.ds(0, 8), thin], send_sem.at[p, 2])
        drain(buf.at[pl.ds(0, 64), wide], send_sem.at[p, 3])
        drain(buf.at[pl.ds(0, 56), thin], send_sem.at[p, 4])
    for j in range(parts):
        drain(core_in.at[1, pl.ds(0, 2), part(j)], ex_send.at[1, j])
        drain(chip_in.at[part(j)], chip_send.at[j])
        drain(pair_in.at[pl.ds(0, 2), part(j)], pair_send.at[j])
    drain(comb.at[pl.ds(0, 2)], cb_send)

    drain(gfin.at[pl.ds(0, 7)], gw_recv.at[2])
    for i in range(8):
        gw_ref[i * PIECE : (i + 1) * PIECE, :] = gfin[i]
    for i in range(3):
        drain(g1.at[pl.ds(0, 7)], gw_send.at[i])


def local(cotangent, features, weight, heat_time, tile_values, tile_row, tile_col, section_offsets):
    vmem = pl.BlockSpec(memory_space=pltpu.VMEM)
    hbm = pl.BlockSpec(memory_space=pl.ANY)
    f32, bf16, i32 = jnp.float32, jnp.bfloat16, jnp.int32
    dma = pltpu.SemaphoreType.DMA
    parts = T // CHUNK
    grad_weight, grad_features = pl.pallas_call(
        kernel,
        out_shape=(
            jax.ShapeDtypeStruct((192, T), f32),
            jax.ShapeDtypeStruct((192, 1024), bf16),
        ),
        in_specs=[hbm, hbm, hbm, pl.BlockSpec(memory_space=pltpu.SMEM), hbm, hbm, hbm, hbm],
        out_specs=(vmem, vmem),
        scratch_shapes=[
            pltpu.SMEM((16,), i32), pltpu.SMEM((16,), i32), pltpu.SMEM((17,), i32),
            pltpu.VMEM((2, T, T), bf16),
            pltpu.VMEM((192, 1024), bf16),
            pltpu.VMEM((192, T), bf16),
            pltpu.VMEM((16, T, T), bf16),
            pltpu.VMEM((RELAY + 16, T, T), bf16),
            pltpu.VMEM((RELAY + 16, T, T), bf16),
            pltpu.VMEM((3, T, T), bf16),
            pltpu.VMEM((4, T, T), f32),
            pltpu.VMEM((2, 2, T, T), f32),
            pltpu.VMEM((T, T), bf16),
            pltpu.VMEM((T, T), bf16),
            pltpu.VMEM((2, T, T), bf16),
            pltpu.VMEM((2, T, T), bf16),
            pltpu.VMEM((4, T, T), bf16),
            pltpu.VMEM((192, T), f32),
            pltpu.VMEM((8, PIECE, T), f32),
            pltpu.VMEM((PIECE, T), f32),
            pltpu.VMEM((8, PIECE, T), f32),
            pltpu.VMEM((PIECE, T), f32),
            pltpu.VMEM((8, PIECE, T), f32),
            dma((3,)), dma((3,)), dma((2,)),
            dma((2,)),
            dma((2, 8, 2)),
            dma((2,)),
            dma((2, 8, 2)),
            dma((2,)),
            dma((2,)),
            dma((2, 8, 2)),
            dma((2, 5)),
            dma((2,)),
            dma((2, parts)), dma((2, parts)),
            dma((parts,)), dma((parts,)),
            dma((parts,)), dma((parts,)),
            dma, dma,
            dma((3,)), dma((3,)),
        ],
        compiler_params=pltpu.CompilerParams(
            collective_id=0, has_side_effects=True, vmem_limit_bytes=60 << 20
        ),
        cost_estimate=pl.CostEstimate(flops=4_800_000_000, bytes_accessed=4_000_000, transcendentals=0),
        name="diffuse",
    )(tile_row, tile_col, section_offsets, heat_time, cotangent, features.T, weight, tile_values)
    return grad_weight, grad_features.T


def solution(mesh):
    in_specs = (
        P("blk", None),
        P("blk", "rep"),
        P("rep", None),
        P(),
        P(("blk", "rep"), None, None),
        P(("blk", "rep")),
        P(("blk", "rep")),
        P(("blk", "rep")),
    )
    out_specs = (P("rep", None), P("blk", "rep"))
    return jax.shard_map(local, mesh=mesh, in_specs=in_specs, out_specs=out_specs, check_vma=False)
```

time: 1350 us -> 168 us (0.12)
  waiting for transfers between devices: 1200 us -> 0 us
  Pallas kernels: 0 us -> 164 us
  local copies, waits for them, and re-layouts: 76.9 us -> 3.38 us
  blocking collectives: 25.9 us -> 0 us
  matrix products: 21.3 us -> 0 us
  between operations: 14.8 us -> 1.29 us
    psum x2 -> x0, waiting for transfers between devices: 675 us -> none  [the longest x1 634 us: local(): grad_weight = lax.psum(partial_weight, 'blk')]
    ppermute x34 -> x0, waiting for transfers between devices: 523 us -> none  [shifted(): lax.ppermute(value, axis, [(i, (i + by) % length) for i in range(length)])]
    pallas_call x0 -> x1, Pallas kernels: none -> 164 us  [local(): pl.pallas_call(kernel, out_shape=(jax.ShapeDtypeStruct((192, T), f32), ja...]
    dynamic_update_slice x32 -> x0, local copies, waits for them, and re-layouts: 33.2 us -> none  [the longest x30 25.1 us: advance(): lax.dynamic_update_index_in_dim(holder, source_block, section_idx, 0)]
    psum x1 -> x0, blocking collectives: 25.9 us -> none  [local(): first = lax.psum(partial_first, 'rep').astype(jnp.bfloat16)]
    dot_general x6 -> x0, matrix products: 21.3 us -> none  [the longest x2 9.58 us: absorb(): jnp.dot(target_table, terms.reshape(slot_count, tile_size * width), preci...]
  transfers between devices with their start and end apart: 36 -> 0, of which waited for: 36 -> 0; matrix products, arithmetic and copies ran while one was open for 1% -> 0% of each run, Pallas kernels for 0% -> 0%
where the time goes in v2:
time: 168 us
  Pallas kernels  164 us (98%)
  local copies, waits for them, and re-layouts  3.38 us (2%)
    pallas_call x1, Pallas kernels, local(): pl.pallas_call(kernel, out_shape=(jax.ShapeDtypeStruct((192, T), f32), ja...  164 us
    unnamed x2, local copies, waits for them, and re-layouts  3.38 us

profile of v2, /device:TPU:2, one launch (start us, length us, event | category | flops | bytes accessed | tf_op | source)
XLA Modules:
  0.0 168.3 jit_solution(10359587876552970310)
XLA Ops:
  1.3 163.6 %diffuse.1 = (f32[192,256]{1,0:T(8,128)}, bf16[192,1024]{1,0:T(8,128)(2,1)}) custom-call(s32[16]{0:T(128)} %rows_hbm.1, s32[16]{0:T(128)} %cols_hbm.1, s32[17]{0:T(128)} %offs_hbm.1, f32[1]{0:T(128)S(6)} %copy.12.heat_ref, bf16[1024,256]{1,0:T(8,128)(2,1)} %cot_hbm.1, bf16[192,1024]{1,0:T(8,128)(2,1)} %bitcast.3, bf16[192,256]{1,0:T(8,128)(2,1)} %weight_hbm.1, ...), custom_call_target="tpu_custom_call" | custom-call | flops 4800000000 | bytes 4000000 | tf_op jit(solution)/shard_map/diffuse/pallas_call | solution.py:410
  164.9 1.6 copy.13
  166.5 1.8 %copy.14 = bf16[1024,192]{0,1:T(8,128)(2,1)} copy(bf16[1024,192]{0,1:T(8,128)(2,1)} %bitcast.2) | data formatting | bytes 786432

commit v3 on v2

--- a/solution.py
+++ b/solution.py
@@ -13,6 +13,35 @@
 CHUNK = 64
 RELAY = 64
 PIECE = 24
+
+FIRST_ORDER = " ".join((
+    "T00 W00 W01 t00",
+    "F00 R00 W10 F01",
+    "W41 W40 W11 R11",
+    "W20 R10 F40 R40",
+    "F11 W50 F41 F10",
+    "W21 W51 F20 F51",
+    "W30 R41 W60 R21",
+    "R20 F50 W31 F21",
+    "W61 W70 R50 R51",
+    "F30 F60 W71 F31",
+    "F61 R31 F71 F70",
+    "R61 R60 R30",
+))
+SECOND_ORDER = " ".join((
+    "T00 t00 W00 W01",
+    "R00 W10 W40 W11",
+    "F01 W41 F10 R40",
+    "R11 F41 R41 F40",
+    "F00 F11 W20 R10",
+    "W21 R50 W50 W51",
+    "W30 R51 F20 F21",
+    "R20 W31 F51 W60",
+    "W61 F30 R21 R61",
+    "F31 R30 W70 R60",
+    "F50 F61 W71 F70",
+    "F71 F60 R31",
+))
 
 
 def xor(a, b):
@@ -26,7 +55,7 @@
     field0, field1, own, acc, core_in, chip_out, chip_in, pair_out, pair_in, comb,
     gwp, g1, s1, g2, s2, gfin,
     load_sem, small_sem, cot_sem,
-    rt_sem, relay_sem, gyt_sem, gy_sem, g0_sem, grest_sem, ring_sem, send_sem, self_sem,
+    rt_sem, relay_sem, thin_sem, plane_sem, ring_sem, send_sem, self_sem,
     ex_send, ex_recv, chip_send, chip_recv, pair_send, pair_recv, cb_send, cb_recv, gw_send, gw_recv,
 ):
     blk = lax.axis_index("blk")
@@ -107,9 +136,8 @@
 
     for device in (y_chain, y_other, x_near, x_far, sibling):
         greet(device)
-    for step in range(1, 8):
-        greet(z_peer(step)[1])
-        greet(plane_peer(step)[1])
+    greet(z_up)
+    greet(z_dn)
 
     def send(src, dst, ssem, rsem, device):
         pltpu.make_async_remote_copy(
@@ -127,7 +155,7 @@
     drain(cot.at[1], cot_sem.at[1])
     own[2] = turned(cot.at[1])
 
-    pl.semaphore_wait(barrier, 22 - one_is_self)
+    pl.semaphore_wait(barrier, 10 - one_is_self)
 
     thin = pl.ds(0, THIN)
     wide = pl.ds(THIN, T - THIN)
@@ -154,7 +182,7 @@
 
         send(two.at[rows], buf.at[slot, rows], send_sem.at[p, 0], sem, to_two)
 
-    def gather(p, buf):
+    def gather(p, buf, order):
         def over_plane(i, tile, count, rows, ssem, chain_sem, rest):
             src = buf.at[pl.ds(RELAY + zp(i) * 2 + tile, count), rows]
             dst = buf.at[pl.ds(spot(i, yr) + tile, count), rows]
@@ -162,12 +190,16 @@
             send(src, dst, ssem, rest, y_other)
             send(src, dst, ssem, rest, x_near)
 
+            @pl.when(n == 0)
+            def _():
+                send(src, dst, ssem, rest, x_far)
+
         def far(i, tile, count, rows, ssem, chain_sem, rest):
-            drain(buf.at[pl.ds(0, count), rows], chain_sem)
-            chained = spot(i, yc) + tile
-            src = (1 - n) * (RELAY + zp(i) * 2 + tile) + n * chained
-            dst = (1 - n) * (spot(i, yr) + tile) + n * chained
-            send(buf.at[pl.ds(src, count), rows], buf.at[pl.ds(dst, count), rows], ssem, rest, x_far)
+            @pl.when(n == 1)
+            def _():
+                drain(buf.at[pl.ds(0, count), rows], chain_sem)
+                part = buf.at[pl.ds(spot(i, yc) + tile, count), rows]
+                send(part, part, ssem, rest, x_far)
 
         def along_z(i, tile, up, follow):
             part = buf.at[RELAY + zp(i) * 2 + tile, wide]
@@ -177,61 +209,60 @@
             part = buf.at[pl.ds(zp(i) * 8 + block * 4, 4), thin]
             send(part, part, send_sem.at[p, 4], ring_sem.at[p, follow, block], z_up if up else z_dn)
 
-        def wide_plane(i, tile):
-            over_plane(i, tile, 1, wide, send_sem.at[p, 3], gy_sem.at[p, i, tile], grest_sem.at[p])
-
-        def wide_far(i):
-            for tile in range(2):
-                far(i, tile, 1, wide, send_sem.at[p, 3], gy_sem.at[p, i, tile], grest_sem.at[p])
-
-        def wide_wait(i, tile):
+        def thin_task():
+            drain(buf.at[pl.ds(0, 2), thin], rt_sem.at[p])
+            over_plane(0, 0, 2, thin, send_sem.at[p, 2], thin_sem.at[p, n], thin_sem.at[p, 0])
+
+        def thin_far_task():
+            far(0, 0, 2, thin, send_sem.at[p, 2], thin_sem.at[p, 1], thin_sem.at[p, 0])
+
+        def wide_task(i, tile):
             drain(buf.at[0, wide], relay_sem.at[p, i, tile])
-
-        def wide_step(s):
-            for tile in range(2):
-                for i, up in ((s, True), (s + 3, False)):
-                    wide_wait(i, tile)
-                    if s < 3 or tile == 1 - up:
-                        along_z(i, tile, up, follow_of[i])
-                    wide_plane(i, tile)
-
-        def thin_step(s):
-            for block in range(2):
-                for i, up in ((s, True), (s + 3, False)):
-                    drain(buf.at[pl.ds(0, 4), thin], ring_sem.at[p, i, block])
-                    if s < 3 or block == 1 - up:
-                        ring(i, block, up, follow_of[i])
-
-        drain(buf.at[pl.ds(0, 2), thin], rt_sem.at[p])
-        over_plane(0, 0, 2, thin, send_sem.at[p, 2], gyt_sem.at[p], g0_sem.at[p])
-        for tile in range(2):
-            wide_wait(0, tile)
-            along_z(0, tile, True, 1)
-            along_z(0, tile, False, 4)
-            wide_plane(0, tile)
-        far(0, 0, 2, thin, send_sem.at[p, 2], gyt_sem.at[p], g0_sem.at[p])
-        drain(buf.at[pl.ds(0, 6), thin], g0_sem.at[p])
-        for block in range(2):
-            ring(0, block, True, 1)
-            ring(0, block, False, 4)
-        wide_step(1)
-        wide_far(0)
-        thin_step(1)
-        wide_step(2)
-        wide_far(1)
-        wide_far(4)
-        thin_step(2)
-        wide_step(3)
-        wide_far(2)
-        wide_far(5)
-        thin_step(3)
-        for tile in range(2):
-            wide_wait(7, tile)
-            wide_plane(7, tile)
-        wide_far(3)
-        wide_far(6)
-        wide_far(7)
-        drain(buf.at[pl.ds(0, 48), wide], grest_sem.at[p])
+            if i == 0:
+                along_z(0, tile, True, 1)
+                along_z(0, tile, False, 4)
+            elif i in (1, 2, 4, 5) or (i, tile) in ((3, 0), (6, 1)):
+                along_z(i, tile, i < 4, follow_of[i])
+            over_plane(
+                i, tile, 1, wide, send_sem.at[p, 3],
+                plane_sem.at[p, n * (1 + i * 2 + tile)], plane_sem.at[p, 0],
+            )
+
+        def wide_far_task(i, tile):
+            far(i, tile, 1, wide, send_sem.at[p, 3], plane_sem.at[p, 1 + i * 2 + tile], plane_sem.at[p, 0])
+
+        def ring_task(i, block):
+            if i == 0:
+                for cls, count in ((0, 8), (1, 6)):
+                    @pl.when(n == cls)
+                    def _(count=count):
+                        drain(buf.at[pl.ds(0, count), thin], thin_sem.at[p, 0])
+
+                for b in range(2):
+                    ring(0, b, True, 1)
+                    ring(0, b, False, 4)
+                return
+            drain(buf.at[pl.ds(0, 4), thin], ring_sem.at[p, i, block])
+            if i in (1, 2, 4, 5) or (i, block) in ((3, 0), (6, 1)):
+                ring(i, block, i < 4, follow_of[i])
+
+        for name in order.split():
+            kind, i, piece = name[0], int(name[1]), int(name[2])
+            if kind == "T":
+                thin_task()
+            elif kind == "t":
+                thin_far_task()
+            elif kind == "W":
+                wide_task(i, piece)
+            elif kind == "F":
+                wide_far_task(i, piece)
+            else:
+                ring_task(i, piece)
+        for cls, count in ((0, 64), (1, 48)):
+            @pl.when(n == cls)
+            def _(count=count):
+                drain(buf.at[pl.ds(0, count), wide], plane_sem.at[p, 0])
+
         for block in range(2):
             drain(buf.at[pl.ds(0, 4), thin], ring_sem.at[p, 7, block])
 
@@ -270,7 +301,7 @@
 
     hand_out(0, field0, thin, relay_two_near, own.at[2])
     hand_out(0, field0, wide, relay_two_near, own.at[2])
-    gather(0, field0)
+    gather(0, field0, FIRST_ORDER)
     for i, ref in enumerate((rows_ref, cols_ref, offs_ref)):
         drain(ref, small_sem.at[i])
     drain(tiles, load_sem.at[0])
@@ -302,7 +333,7 @@
     close_first(parts - 1)
 
     hand_out(1, field1, wide, relay_two, own.at[1])
-    gather(1, field1)
+    gather(1, field1, SECOND_ORDER)
     for j in range(parts):
         drain(core_in.at[0, pl.ds(0, 2), part(j)], ex_send.at[0, j])
 
@@ -354,13 +385,15 @@
             feat[:, t * T : (t + 1) * T], comb[t], (((1,), (1,)), ((), ())),
             preferred_element_type=jnp.float32,
         )
-    gwp[...] = partial * (1.0 / 256.0)
+    partial = partial * (1.0 / 256.0)
+    for i in range(8):
+        piece = partial[i * PIECE : (i + 1) * PIECE]
+        gwp[i] = jnp.concatenate([piece[:, :128], piece[:, 128:]], axis=0).astype(jnp.bfloat16)
 
     for step in range(1, 8):
         place, device = plane_peer(step)
-        rows = pl.ds(pl.multiple_of(place * PIECE, 8), PIECE)
-        send(gwp.at[rows], g1.at[here], gw_send.at[0], gw_recv.at[0], device)
-    g1[here] = gwp[pl.ds(pl.multiple_of(here * PIECE, 8), PIECE), :]
+        send(gwp.at[place], g1.at[here], gw_send.at[0], gw_recv.at[0], device)
+    g1[here] = gwp[here]
 
     for t in range(4):
         gf_ref[:, t * T : (t + 1) * T] = jnp.dot(
@@ -368,12 +401,14 @@
         ).astype(jnp.bfloat16)
 
     drain(g1.at[pl.ds(0, 7)], gw_recv.at[0])
-    s1[...] = functools.reduce(lambda a, b: a + b, [g1[i] for i in range(8)])
+    s1[...] = functools.reduce(lambda a, b: a + b, [g1[i].astype(jnp.float32) for i in range(8)]).astype(
+        jnp.bfloat16
+    )
     for step in range(1, 8):
         send(s1, g2.at[z], gw_send.at[1], gw_recv.at[1], z_peer(step)[1])
     g2[z] = s1[...]
     drain(g2.at[pl.ds(0, 7)], gw_recv.at[1])
-    s2[...] = functools.reduce(lambda a, b: a + b, [g2[i] for i in range(8)])
+    s2[...] = functools.reduce(lambda a, b: a + b, [g2[i].astype(jnp.float32) for i in range(8)])
     for step in range(1, 8):
         send(s2, gfin.at[here], gw_send.at[2], gw_recv.at[2], plane_peer(step)[1])
     gfin[here] = s2[...]
@@ -396,14 +431,26 @@
 
     drain(gfin.at[pl.ds(0, 7)], gw_recv.at[2])
     for i in range(8):
-        gw_ref[i * PIECE : (i + 1) * PIECE, :] = gfin[i]
-    for i in range(3):
-        drain(g1.at[pl.ds(0, 7)], gw_send.at[i])
+        gw_ref[i * PIECE : (i + 1) * PIECE, :128] = gfin[i, :PIECE, :]
+        gw_ref[i * PIECE : (i + 1) * PIECE, 128:] = gfin[i, PIECE:, :]
+    for i, ref in enumerate((g1, g2, gfin)):
+        drain(ref.at[pl.ds(0, 7)], gw_send.at[i])
+
+
+def hand_back(gw_in, gf_in, gw_out, gf_out, sem):
+    copies = [
+        pltpu.make_async_copy(src, dst, sem.at[i])
+        for i, (src, dst) in enumerate(((gw_in, gw_out), (gf_in, gf_out)))
+    ]
+    for copy in copies:
+        copy.start()
+    for copy in copies:
+        copy.wait()
 
 
 def local(cotangent, features, weight, heat_time, tile_values, tile_row, tile_col, section_offsets):
     vmem = pl.BlockSpec(memory_space=pltpu.VMEM)
-    hbm = pl.BlockSpec(memory_space=pl.ANY)
+    hbm = pl.BlockSpec(memory_space=pltpu.HBM)
     f32, bf16, i32 = jnp.float32, jnp.bfloat16, jnp.int32
     dma = pltpu.SemaphoreType.DMA
     parts = T // CHUNK
@@ -431,19 +478,17 @@
             pltpu.VMEM((2, T, T), bf16),
             pltpu.VMEM((2, T, T), bf16),
             pltpu.VMEM((4, T, T), bf16),
-            pltpu.VMEM((192, T), f32),
-            pltpu.VMEM((8, PIECE, T), f32),
-            pltpu.VMEM((PIECE, T), f32),
-            pltpu.VMEM((8, PIECE, T), f32),
-            pltpu.VMEM((PIECE, T), f32),
-            pltpu.VMEM((8, PIECE, T), f32),
+            pltpu.VMEM((8, 2 * PIECE, 128), bf16),
+            pltpu.VMEM((8, 2 * PIECE, 128), bf16),
+            pltpu.VMEM((2 * PIECE, 128), bf16),
+            pltpu.VMEM((8, 2 * PIECE, 128), bf16),
+            pltpu.VMEM((2 * PIECE, 128), f32),
+            pltpu.VMEM((8, 2 * PIECE, 128), f32),
             dma((3,)), dma((3,)), dma((2,)),
             dma((2,)),
             dma((2, 8, 2)),
-            dma((2,)),
-            dma((2, 8, 2)),
-            dma((2,)),
-            dma((2,)),
+            dma((2, 2)),
+            dma((2, 17)),
             dma((2, 8, 2)),
             dma((2, 5)),
             dma((2,)),
@@ -459,6 +504,17 @@
         cost_estimate=pl.CostEstimate(flops=4_800_000_000, bytes_accessed=4_000_000, transcendentals=0),
         name="diffuse",
     )(tile_row, tile_col, section_offsets, heat_time, cotangent, features.T, weight, tile_values)
+    grad_weight, grad_features = pl.pallas_call(
+        hand_back,
+        out_shape=(
+            jax.ShapeDtypeStruct((192, T), f32),
+            jax.ShapeDtypeStruct((192, 1024), bf16),
+        ),
+        in_specs=[pl.BlockSpec(memory_space=pl.ANY)] * 2,
+        out_specs=(pl.BlockSpec(memory_space=pl.ANY),) * 2,
+        scratch_shapes=[dma((2,))],
+        name="hand_back",
+    )(grad_weight, grad_features)
     return grad_weight, grad_features.T
 
 

time: 168 us -> 167 us (level)
  local copies, waits for them, and re-layouts: 3.38 us -> 0 us
    pallas_call x0 -> x1, Pallas kernels: none -> 19 us  [local(): pl.pallas_call(hand_back, out_shape=(jax.ShapeDtypeStruct((192, T), f32),...]
    pallas_call x1, Pallas kernels: 164 us -> 146 us  [local(): pl.pallas_call(kernel, out_shape=(jax.ShapeDtypeStruct((192, T), f32), ja...]
    unnamed x2 -> x0, local copies, waits for them, and re-layouts: 3.38 us -> none
where the time goes in v3:
time: 167 us; the launch traced here: 166 us
  Pallas kernels  165 us (99%)
    pallas_call x1, Pallas kernels, local(): pl.pallas_call(kernel, out_shape=(jax.ShapeDtypeStruct((192, T), f32), ja...  146 us
    pallas_call x1, Pallas kernels, local(): pl.pallas_call(hand_back, out_shape=(jax.ShapeDtypeStruct((192, T), f32),...  19 us

profile of v3, /device:TPU:2, one launch (start us, length us, event | category | flops | bytes accessed | tf_op | source)
XLA Modules:
  0.0 166.5 jit_solution(9772698196754365534)
XLA Ops:
  1.3 146.2 %diffuse.1 = (f32[192,256]{1,0:T(8,128)}, bf16[192,1024]{1,0:T(8,128)(2,1)}) custom-call(s32[16]{0:T(128)} %rows_hbm.1, s32[16]{0:T(128)} %cols_hbm.1, s32[17]{0:T(128)} %offs_hbm.1, f32[1]{0:T(128)S(6)} %copy.10.heat_ref, bf16[1024,256]{1,0:T(8,128)(2,1)} %cot_hbm.1, bf16[192,1024]{1,0:T(8,128)(2,1)} %bitcast.2, bf16[192,256]{1,0:T(8,128)(2,1)} %weight_hbm.1, ...), custom_call_target="tpu_custom_call" | custom-call | flops 4800000000 | bytes 4000000 | tf_op jit(solution)/shard_map/diffuse/pallas_call | solution.py:457
  147.5 19.0 %hand_back.1 = (f32[192,256]{1,0:T(8,128)}, bf16[192,1024]{1,0:T(8,128)(2,1)}) custom-call(f32[192,256]{1,0:T(8,128)} %get-tuple-element.6.gw_in, bf16[192,1024]{1,0:T(8,128)(2,1)} %get-tuple-element.7.gf_in), custom_call_target="tpu_custom_call" | custom-call | tf_op jit(solution)/shard_map/hand_back/pallas_call | solution.py:507

commit v4 on v3

--- a/solution.py
+++ b/solution.py
@@ -322,17 +322,14 @@
     for j in range(parts):
         products(field0, j)
         swap_cores(0, j)
-        if j >= 1:
-            pass_on(j - 1)
         if j >= 2:
-            close_first(j - 2)
-        if j == 2:
-            hand_out(1, field1, thin, relay_two, own.at[1])
+            pass_on(j - 2)
+    pass_on(parts - 2)
     pass_on(parts - 1)
-    close_first(parts - 2)
-    close_first(parts - 1)
-
-    hand_out(1, field1, wide, relay_two, own.at[1])
+    for j in range(parts):
+        close_first(j)
+        hand_out(1, field1, thin if j == 0 else part(j), relay_two, own.at[1])
+
     gather(1, field1, SECOND_ORDER)
     for j in range(parts):
         drain(core_in.at[0, pl.ds(0, 2), part(j)], ex_send.at[0, j])
@@ -368,13 +365,12 @@
     for j in range(parts):
         products(field1, j)
         swap_cores(1, j)
-        if j >= 1:
-            pair_up(j - 1)
         if j >= 2:
-            close_second(j - 2)
+            pair_up(j - 2)
+    pair_up(parts - 2)
     pair_up(parts - 1)
-    close_second(parts - 2)
-    close_second(parts - 1)
+    for j in range(parts):
+        close_second(j)
     drain(feat, load_sem.at[1])
     drain(weight, load_sem.at[2])
     drain(comb.at[pl.ds(0, 2)], cb_recv)
@@ -437,15 +433,9 @@
         drain(ref.at[pl.ds(0, 7)], gw_send.at[i])
 
 
-def hand_back(gw_in, gf_in, gw_out, gf_out, sem):
-    copies = [
-        pltpu.make_async_copy(src, dst, sem.at[i])
-        for i, (src, dst) in enumerate(((gw_in, gw_out), (gf_in, gf_out)))
-    ]
-    for copy in copies:
-        copy.start()
-    for copy in copies:
-        copy.wait()
+def hand_back(gw_in, gf_in, gw_out, gf_out):
+    gw_out[...] = gw_in[...]
+    gf_out[...] = gf_in[...]
 
 
 def local(cotangent, features, weight, heat_time, tile_values, tile_row, tile_col, section_offsets):
@@ -510,9 +500,8 @@
             jax.ShapeDtypeStruct((192, T), f32),
             jax.ShapeDtypeStruct((192, 1024), bf16),
         ),
-        in_specs=[pl.BlockSpec(memory_space=pl.ANY)] * 2,
-        out_specs=(pl.BlockSpec(memory_space=pl.ANY),) * 2,
-        scratch_shapes=[dma((2,))],
+        in_specs=[vmem, vmem],
+        out_specs=(vmem, vmem),
         name="hand_back",
     )(grad_weight, grad_features)
     return grad_weight, grad_features.T

time: 167 us -> 147 us (0.88)
  Pallas kernels: 165 us -> 145 us
    pallas_call x1, Pallas kernels: 19 us -> 1.93 us  [local(): pl.pallas_call(hand_back, out_shape=(jax.ShapeDtypeStruct((192, T), f32),...]
    pallas_call x1, Pallas kernels: 146 us -> 143 us  [local(): pl.pallas_call(kernel, out_shape=(jax.ShapeDtypeStruct((192, T), f32), ja...]
where the time goes in v4:
time: 147 us; the launch traced here: 146 us
  Pallas kernels  145 us (99%)
    pallas_call x1, Pallas kernels, local(): pl.pallas_call(kernel, out_shape=(jax.ShapeDtypeStruct((192, T), f32), ja...  143 us

profile of v4, /device:TPU:2, one launch (start us, length us, event | category | flops | bytes accessed | tf_op | source)
XLA Modules:
  0.0 146.5 jit_solution(10404488715223658958)
XLA Ops:
  1.3 143.3 %diffuse.1 = (f32[192,256]{1,0:T(8,128)}, bf16[192,1024]{1,0:T(8,128)(2,1)}) custom-call(s32[16]{0:T(128)} %rows_hbm.1, s32[16]{0:T(128)} %cols_hbm.1, s32[17]{0:T(128)} %offs_hbm.1, f32[1]{0:T(128)S(6)} %copy.10.heat_ref, bf16[1024,256]{1,0:T(8,128)(2,1)} %cot_hbm.1, bf16[192,1024]{1,0:T(8,128)(2,1)} %bitcast.2, bf16[192,256]{1,0:T(8,128)(2,1)} %weight_hbm.1, ...), custom_call_target="tpu_custom_call" | custom-call | flops 4800000000 | bytes 4000000 | tf_op jit(solution)/shard_map/diffuse/pallas_call | solution.py:447
  144.5 1.9 %hand_back.1 = (f32[192,256]{1,0:T(8,128)}, bf16[192,1024]{1,0:T(8,128)(2,1)}) custom-call(f32[192,256]{1,0:T(8,128)} %get-tuple-element.6.gw_in, bf16[192,1024]{1,0:T(8,128)(2,1)} %get-tuple-element.7.gf_in), custom_call_target="tpu_custom_call" | custom-call | tf_op jit(solution)/shard_map/hand_back/pallas_call | solution.py:497

commit v5 on v4

--- a/solution.py
+++ b/solution.py
@@ -10,37 +10,37 @@
 MESH = pl.DeviceIdType.MESH
 T = 256
 THIN = 64
-CHUNK = 64
+CHUNK = THIN
 RELAY = 64
 PIECE = 24
 
 FIRST_ORDER = " ".join((
     "T00 W00 W01 t00",
-    "F00 R00 W10 F01",
-    "W41 W40 W11 R11",
-    "W20 R10 F40 R40",
-    "F11 W50 F41 F10",
-    "W21 W51 F20 F51",
-    "W30 R41 W60 R21",
-    "R20 F50 W31 F21",
-    "W61 W70 R50 R51",
-    "F30 F60 W71 F31",
-    "F61 R31 F71 F70",
-    "R61 R60 R30",
+    "W10 W41 F00 W11",
+    "W40 F01 R00 W20",
+    "F10 W51 F40 W21",
+    "W50 F41 F11 R11",
+    "R40 R10 F51 W30",
+    "R41 W61 F20 F21",
+    "W31 F50 W60 F30",
+    "R20 F61 R51 W70",
+    "F31 R21 R50 W71",
+    "F60 F70 F71 R31",
+    "R61 R30 R60",
 ))
 SECOND_ORDER = " ".join((
-    "T00 t00 W00 W01",
-    "R00 W10 W40 W11",
-    "F01 W41 F10 R40",
-    "R11 F41 R41 F40",
-    "F00 F11 W20 R10",
-    "W21 R50 W50 W51",
-    "W30 R51 F20 F21",
-    "R20 W31 F51 W60",
-    "W61 F30 R21 R61",
-    "F31 R30 W70 R60",
-    "F50 F61 W71 F70",
-    "F71 F60 R31",
+    "W01 W00 T00 W41",
+    "W10 W11 t00 F01",
+    "W51 F00 W40 W20",
+    "R00 F41 F10 W61",
+    "W30 W21 F40 F20",
+    "F51 F11 R40 R10",
+    "W50 F30 W71 F61",
+    "R11 F21 R41 W70",
+    "F50 R50 W31 F71",
+    "R20 W60 F70 R51",
+    "R21 F31 F60 R30",
+    "R61 R60 R31",
 ))
 
 
@@ -52,7 +52,7 @@
     rows_hbm, cols_hbm, offs_hbm, heat_ref, cot_hbm, feat_hbm, weight_hbm, tiles_hbm,
     gw_ref, gf_ref,
     rows_ref, cols_ref, offs_ref, cot, feat, weight, tiles,
-    field0, field1, own, acc, core_in, chip_out, chip_in, pair_out, pair_in, comb,
+    wide0, thin0, wide1, thin1, own, acc, core_in, chip_out, chip_in, pair_out, pair_in, comb,
     gwp, g1, s1, g2, s2, gfin,
     load_sem, small_sem, cot_sem,
     rt_sem, relay_sem, thin_sem, plane_sem, ring_sem, send_sem, self_sem,
@@ -157,8 +157,11 @@
 
     pl.semaphore_wait(barrier, 10 - one_is_self)
 
-    thin = pl.ds(0, THIN)
-    wide = pl.ds(THIN, T - THIN)
+    parts = T // CHUNK
+
+    def part(j):
+        return pl.ds(j * CHUNK, CHUNK)
+
     follow_of = {1: 2, 2: 3, 3: 7, 4: 5, 5: 6, 6: 7}
 
     def zp(i):
@@ -167,25 +170,28 @@
     def spot(i, ysrc):
         return (zp(i) * 2 + ysrc // 2) * 4 + hr * 2
 
-    def hand_out(p, buf, rows, to_two, two):
-        mine = own.at[p, rows]
+    def hand_out(p, thin_buf, wide_buf, j, to_two, two):
+        mine = own.at[p, part(j)]
         slot = RELAY + z * 2 + c
-        sem = rt_sem.at[p] if rows is thin else relay_sem.at[p, 0, c]
+        if j == 0:
+            place, sem = thin_buf.at[slot], rt_sem.at[p]
+        else:
+            place, sem = wide_buf.at[slot, part(j - 1)], relay_sem.at[p, 0, c]
 
         @pl.when(one_is_self == 1)
         def _():
-            load(mine, buf.at[slot, rows], sem)
+            load(mine, place, sem)
 
         @pl.when(one_is_self == 0)
         def _():
-            send(mine, buf.at[slot, rows], self_sem.at[p], sem, relay_one)
-
-        send(two.at[rows], buf.at[slot, rows], send_sem.at[p, 0], sem, to_two)
-
-    def gather(p, buf, order):
-        def over_plane(i, tile, count, rows, ssem, chain_sem, rest):
-            src = buf.at[pl.ds(RELAY + zp(i) * 2 + tile, count), rows]
-            dst = buf.at[pl.ds(spot(i, yr) + tile, count), rows]
+            send(mine, place, self_sem.at[p], sem, relay_one)
+
+        send(two.at[part(j)], place, send_sem.at[p, 0], sem, to_two)
+
+    def gather(p, thin_buf, wide_buf, order):
+        def over_plane(buf, i, tile, count, ssem, chain_sem, rest):
+            src = buf.at[pl.ds(RELAY + zp(i) * 2 + tile, count)]
+            dst = buf.at[pl.ds(spot(i, yr) + tile, count)]
             send(src, dst, ssem, chain_sem, y_chain)
             send(src, dst, ssem, rest, y_other)
             send(src, dst, ssem, rest, x_near)
@@ -194,55 +200,55 @@
             def _():
                 send(src, dst, ssem, rest, x_far)
 
-        def far(i, tile, count, rows, ssem, chain_sem, rest):
+        def far(buf, i, tile, count, ssem, chain_sem, rest):
             @pl.when(n == 1)
             def _():
-                drain(buf.at[pl.ds(0, count), rows], chain_sem)
-                part = buf.at[pl.ds(spot(i, yc) + tile, count), rows]
-                send(part, part, ssem, rest, x_far)
+                drain(buf.at[pl.ds(0, count)], chain_sem)
+                place = buf.at[pl.ds(spot(i, yc) + tile, count)]
+                send(place, place, ssem, rest, x_far)
 
         def along_z(i, tile, up, follow):
-            part = buf.at[RELAY + zp(i) * 2 + tile, wide]
-            send(part, part, send_sem.at[p, 1], relay_sem.at[p, follow, tile], z_up if up else z_dn)
+            place = wide_buf.at[RELAY + zp(i) * 2 + tile]
+            send(place, place, send_sem.at[p, 1], relay_sem.at[p, follow, tile], z_up if up else z_dn)
 
         def ring(i, block, up, follow):
-            part = buf.at[pl.ds(zp(i) * 8 + block * 4, 4), thin]
-            send(part, part, send_sem.at[p, 4], ring_sem.at[p, follow, block], z_up if up else z_dn)
+            place = thin_buf.at[pl.ds(zp(i) * 8 + block * 4, 4)]
+            send(place, place, send_sem.at[p, 4], ring_sem.at[p, follow, block], z_up if up else z_dn)
 
         def thin_task():
-            drain(buf.at[pl.ds(0, 2), thin], rt_sem.at[p])
-            over_plane(0, 0, 2, thin, send_sem.at[p, 2], thin_sem.at[p, n], thin_sem.at[p, 0])
+            drain(thin_buf.at[pl.ds(0, 2)], rt_sem.at[p])
+            over_plane(thin_buf, 0, 0, 2, send_sem.at[p, 2], thin_sem.at[p, n], thin_sem.at[p, 0])
 
         def thin_far_task():
-            far(0, 0, 2, thin, send_sem.at[p, 2], thin_sem.at[p, 1], thin_sem.at[p, 0])
+            far(thin_buf, 0, 0, 2, send_sem.at[p, 2], thin_sem.at[p, 1], thin_sem.at[p, 0])
 
         def wide_task(i, tile):
-            drain(buf.at[0, wide], relay_sem.at[p, i, tile])
+            drain(wide_buf.at[0], relay_sem.at[p, i, tile])
             if i == 0:
                 along_z(0, tile, True, 1)
                 along_z(0, tile, False, 4)
             elif i in (1, 2, 4, 5) or (i, tile) in ((3, 0), (6, 1)):
                 along_z(i, tile, i < 4, follow_of[i])
             over_plane(
-                i, tile, 1, wide, send_sem.at[p, 3],
+                wide_buf, i, tile, 1, send_sem.at[p, 3],
                 plane_sem.at[p, n * (1 + i * 2 + tile)], plane_sem.at[p, 0],
             )
 
         def wide_far_task(i, tile):
-            far(i, tile, 1, wide, send_sem.at[p, 3], plane_sem.at[p, 1 + i * 2 + tile], plane_sem.at[p, 0])
+            far(wide_buf, i, tile, 1, send_sem.at[p, 3], plane_sem.at[p, 1 + i * 2 + tile], plane_sem.at[p, 0])
 
         def ring_task(i, block):
             if i == 0:
                 for cls, count in ((0, 8), (1, 6)):
                     @pl.when(n == cls)
                     def _(count=count):
-                        drain(buf.at[pl.ds(0, count), thin], thin_sem.at[p, 0])
+                        drain(thin_buf.at[pl.ds(0, count)], thin_sem.at[p, 0])
 
                 for b in range(2):
                     ring(0, b, True, 1)
                     ring(0, b, False, 4)
                 return
-            drain(buf.at[pl.ds(0, 4), thin], ring_sem.at[p, i, block])
+            drain(thin_buf.at[pl.ds(0, 4)], ring_sem.at[p, i, block])
             if i in (1, 2, 4, 5) or (i, block) in ((3, 0), (6, 1)):
                 ring(i, block, i < 4, follow_of[i])
 
@@ -261,24 +267,21 @@
         for cls, count in ((0, 64), (1, 48)):
             @pl.when(n == cls)
             def _(count=count):
-                drain(buf.at[pl.ds(0, count), wide], plane_sem.at[p, 0])
-
+                drain(wide_buf.at[pl.ds(0, count)], plane_sem.at[p, 0])
+
+    def last_thin(p, thin_buf):
         for block in range(2):
-            drain(buf.at[pl.ds(0, 4), thin], ring_sem.at[p, 7, block])
-
-    def part(j):
-        return pl.ds(j * CHUNK, CHUNK)
-
-    parts = T // CHUNK
-
-    def products(buf, j):
+            drain(thin_buf.at[pl.ds(0, 4)], ring_sem.at[p, 7, block])
+
+    def products(thin_buf, wide_buf, j):
         rows = part(j)
         total = jnp.zeros((4 * CHUNK, T), jnp.float32)
         for k in range(16):
             row = rows_ref[k]
             col = cols_ref[k] % 4
             alive = k < offs_ref[16]
-            tile = buf[((row // 16) % 16) * 4 + row % 4, rows, :]
+            index = ((row // 16) % 16) * 4 + row % 4
+            tile = thin_buf[index] if j == 0 else wide_buf[index, part(j - 1), :]
             picked = [
                 jnp.where(jnp.logical_and(col == t, alive), tile, jnp.zeros_like(tile)) for t in range(4)
             ]
@@ -299,9 +302,9 @@
     def await_cores(p, j):
         drain(core_in.at[p, pl.ds(0, 2), part(j)], ex_recv.at[p, j])
 
-    hand_out(0, field0, thin, relay_two_near, own.at[2])
-    hand_out(0, field0, wide, relay_two_near, own.at[2])
-    gather(0, field0, FIRST_ORDER)
+    for j in range(parts):
+        hand_out(0, thin0, wide0, j, relay_two_near, own.at[2])
+    gather(0, thin0, wide0, FIRST_ORDER)
     for i, ref in enumerate((rows_ref, cols_ref, offs_ref)):
         drain(ref, small_sem.at[i])
     drain(tiles, load_sem.at[0])
@@ -319,18 +322,22 @@
             acc[own_tile, rows, :] + core_in[0, hx, rows, :] + chip_in[rows, :].astype(jnp.float32)
         ).astype(jnp.bfloat16)
 
-    for j in range(parts):
-        products(field0, j)
+    for j in range(1, parts):
+        products(thin0, wide0, j)
         swap_cores(0, j)
-        if j >= 2:
-            pass_on(j - 2)
-    pass_on(parts - 2)
-    pass_on(parts - 1)
-    for j in range(parts):
+    for j in range(1, parts):
+        pass_on(j)
+    last_thin(0, thin0)
+    products(thin0, wide0, 0)
+    swap_cores(0, 0)
+    for j in range(1, parts):
         close_first(j)
-        hand_out(1, field1, thin if j == 0 else part(j), relay_two, own.at[1])
-
-    gather(1, field1, SECOND_ORDER)
+        hand_out(1, thin1, wide1, j, relay_two, own.at[1])
+    pass_on(0)
+    close_first(0)
+    hand_out(1, thin1, wide1, 0, relay_two, own.at[1])
+
+    gather(1, thin1, wide1, SECOND_ORDER)
     for j in range(parts):
         drain(core_in.at[0, pl.ds(0, 2), part(j)], ex_send.at[0, j])
 
@@ -362,15 +369,18 @@
             )
             send(comb.at[tile, rows], comb.at[tile, rows], cb_send, cb_recv, sibling)
 
-    for j in range(parts):
-        products(field1, j)
+    for j in range(1, parts):
+        products(thin1, wide1, j)
         swap_cores(1, j)
-        if j >= 2:
-            pair_up(j - 2)
-    pair_up(parts - 2)
-    pair_up(parts - 1)
-    for j in range(parts):
+    for j in range(1, parts):
+        pair_up(j)
+    last_thin(1, thin1)
+    products(thin1, wide1, 0)
+    swap_cores(1, 0)
+    for j in range(1, parts):
         close_second(j)
+    pair_up(0)
+    close_second(0)
     drain(feat, load_sem.at[1])
     drain(weight, load_sem.at[2])
     drain(comb.at[pl.ds(0, 2)], cb_recv)
@@ -409,16 +419,16 @@
         send(s2, gfin.at[here], gw_send.at[2], gw_recv.at[2], plane_peer(step)[1])
     gfin[here] = s2[...]
 
-    for p, buf in enumerate((field0, field1)):
+    for p, (thin_buf, wide_buf) in enumerate(((thin0, wide0), (thin1, wide1))):
         @pl.when(one_is_self == 0)
         def _(p=p):
             drain(own.at[p], self_sem.at[p])
 
         drain(own.at[p], send_sem.at[p, 0])
-        drain(buf.at[pl.ds(0, 14), wide], send_sem.at[p, 1])
-        drain(buf.at[pl.ds(0, 8), thin], send_sem.at[p, 2])
-        drain(buf.at[pl.ds(0, 64), wide], send_sem.at[p, 3])
-        drain(buf.at[pl.ds(0, 56), thin], send_sem.at[p, 4])
+        drain(wide_buf.at[pl.ds(0, 14)], send_sem.at[p, 1])
+        drain(thin_buf.at[pl.ds(0, 8)], send_sem.at[p, 2])
+        drain(wide_buf.at[pl.ds(0, 64)], send_sem.at[p, 3])
+        drain(thin_buf.at[pl.ds(0, 56)], send_sem.at[p, 4])
     for j in range(parts):
         drain(core_in.at[1, pl.ds(0, 2), part(j)], ex_send.at[1, j])
         drain(chip_in.at[part(j)], chip_send.at[j])
@@ -458,8 +468,10 @@
             pltpu.VMEM((192, 1024), bf16),
             pltpu.VMEM((192, T), bf16),
             pltpu.VMEM((16, T, T), bf16),
-            pltpu.VMEM((RELAY + 16, T, T), bf16),
-            pltpu.VMEM((RELAY + 16, T, T), bf16),
+            pltpu.VMEM((RELAY + 16, T - THIN, T), bf16),
+            pltpu.VMEM((RELAY + 16, THIN, T), bf16),
+            pltpu.VMEM((RELAY + 16, T - THIN, T), bf16),
+            pltpu.VMEM((RELAY + 16, THIN, T), bf16),
             pltpu.VMEM((3, T, T), bf16),
             pltpu.VMEM((4, T, T), f32),
             pltpu.VMEM((2, 2, T, T), f32),

time: 147 us -> 141 us (0.959); the launches traced: 146 us -> 139 us
  Pallas kernels: 145 us -> 138 us
    pallas_call x1, Pallas kernels: 143 us -> 136 us  [local(): pl.pallas_call(kernel, out_shape=(jax.ShapeDtypeStruct((192, T), f32), ja...]
where the time goes in v5:
time: 141 us; the launch traced here: 139 us
  Pallas kernels  138 us (98%)
    pallas_call x1, Pallas kernels, local(): pl.pallas_call(kernel, out_shape=(jax.ShapeDtypeStruct((192, T), f32), ja...  136 us

profile of v5, /device:TPU:2, one launch (start us, length us, event | category | flops | bytes accessed | tf_op | source)
XLA Modules:
  0.0 139.0 jit_solution(6315866586510898007)
XLA Ops:
  1.3 135.8 %diffuse.1 = (f32[192,256]{1,0:T(8,128)}, bf16[192,1024]{1,0:T(8,128)(2,1)}) custom-call(s32[16]{0:T(128)} %rows_hbm.1, s32[16]{0:T(128)} %cols_hbm.1, s32[17]{0:T(128)} %offs_hbm.1, f32[1]{0:T(128)S(6)} %copy.10.heat_ref, bf16[1024,256]{1,0:T(8,128)(2,1)} %cot_hbm.1, bf16[192,1024]{1,0:T(8,128)(2,1)} %bitcast.2, bf16[192,256]{1,0:T(8,128)(2,1)} %weight_hbm.1, ...), custom_call_target="tpu_custom_call" | custom-call | flops 4800000000 | bytes 4000000 | tf_op jit(solution)/shard_map/diffuse/pallas_call | solution.py:457
  137.0 1.9 %hand_back.1 = (f32[192,256]{1,0:T(8,128)}, bf16[192,1024]{1,0:T(8,128)(2,1)}) custom-call(f32[192,256]{1,0:T(8,128)} %get-tuple-element.6.gw_in, bf16[192,1024]{1,0:T(8,128)(2,1)} %get-tuple-element.7.gf_in), custom_call_target="tpu_custom_call" | custom-call | tf_op jit(solution)/shard_map/hand_back/pallas_call | solution.py:509

commit v6 on v5

--- a/solution.py
+++ b/solution.py
@@ -9,38 +9,48 @@
 
 MESH = pl.DeviceIdType.MESH
 T = 256
-THIN = 64
-CHUNK = THIN
+THIN = 80
+BOUNDS = (0, 80, 160, 256)
 RELAY = 64
+PLANE_STEPS = (3, 5, 1, 7, 4, 2, 6)
+Z_STEPS = (4, 3, 5, 2, 6, 1, 7)
 PIECE = 24
 
 FIRST_ORDER = " ".join((
-    "T00 W00 W01 t00",
-    "W10 W41 F00 W11",
-    "W40 F01 R00 W20",
-    "F10 W51 F40 W21",
-    "W50 F41 F11 R11",
-    "R40 R10 F51 W30",
-    "R41 W61 F20 F21",
-    "W31 F50 W60 F30",
-    "R20 F61 R51 W70",
-    "F31 R21 R50 W71",
-    "F60 F70 F71 R31",
-    "R61 R30 R60",
+    "T00 W01 P01 W00",
+    "P00 t00 W41 F01",
+    "W11 W10 W40 P41",
+    "P10 P11 P40 F00",
+    "R00 F41 F40 W20",
+    "W50 W51 P51 F11",
+    "P50 W21 F10 P20",
+    "P21 R41 R10 W30",
+    "P30 W61 F21 P61",
+    "W60 R40 F20 F51",
+    "P60 F50 W31 R11",
+    "P31 W71 P71 R20",
+    "F30 F61 R51 R50",
+    "W70 F60 P70 F31",
+    "R21 F71 F70 R60",
+    "R61 R30 R31",
 ))
 SECOND_ORDER = " ".join((
-    "W01 W00 T00 W41",
-    "W10 W11 t00 F01",
-    "W51 F00 W40 W20",
-    "R00 F41 F10 W61",
-    "W30 W21 F40 F20",
-    "F51 F11 R40 R10",
-    "W50 F30 W71 F61",
-    "R11 F21 R41 W70",
-    "F50 R50 W31 F71",
-    "R20 W60 F70 R51",
-    "R21 F31 F60 R30",
-    "R61 R60 R31",
+    "W01 W00 P01 T00",
+    "W11 W41 P41 W40",
+    "W10 P10 F01 P00",
+    "W51 W21 t00 F10",
+    "P21 P40 W50 W20",
+    "R00 F41 F00 P20",
+    "P51 F21 F40 W30",
+    "W61 P30 W60 P60",
+    "W31 R10 R41 F20",
+    "R40 R11 F51 P61",
+    "P11 F30 P31 W70",
+    "F60 F61 P70 R51",
+    "F11 P50 W71 R21",
+    "R50 P71 R20 F31",
+    "F70 F50 F71 R31",
+    "R60 R61 R30",
 ))
 
 
@@ -157,10 +167,13 @@
 
     pl.semaphore_wait(barrier, 10 - one_is_self)
 
-    parts = T // CHUNK
+    parts = len(BOUNDS) - 1
 
     def part(j):
-        return pl.ds(j * CHUNK, CHUNK)
+        return pl.ds(BOUNDS[j], BOUNDS[j + 1] - BOUNDS[j])
+
+    def wide_part(j):
+        return pl.ds(BOUNDS[j] - THIN, BOUNDS[j + 1] - BOUNDS[j])
 
     follow_of = {1: 2, 2: 3, 3: 7, 4: 5, 5: 6, 6: 7}
 
@@ -176,7 +189,7 @@
         if j == 0:
             place, sem = thin_buf.at[slot], rt_sem.at[p]
         else:
-            place, sem = wide_buf.at[slot, part(j - 1)], relay_sem.at[p, 0, c]
+            place, sem = wide_buf.at[slot, wide_part(j)], relay_sem.at[p, 0, c]
 
         @pl.when(one_is_self == 1)
         def _():
@@ -229,6 +242,8 @@
                 along_z(0, tile, False, 4)
             elif i in (1, 2, 4, 5) or (i, tile) in ((3, 0), (6, 1)):
                 along_z(i, tile, i < 4, follow_of[i])
+
+        def wide_plane_task(i, tile):
             over_plane(
                 wide_buf, i, tile, 1, send_sem.at[p, 3],
                 plane_sem.at[p, n * (1 + i * 2 + tile)], plane_sem.at[p, 0],
@@ -260,6 +275,8 @@
                 thin_far_task()
             elif kind == "W":
                 wide_task(i, piece)
+            elif kind == "P":
+                wide_plane_task(i, piece)
             elif kind == "F":
                 wide_far_task(i, piece)
             else:
@@ -275,13 +292,14 @@
 
     def products(thin_buf, wide_buf, j):
         rows = part(j)
-        total = jnp.zeros((4 * CHUNK, T), jnp.float32)
+        size = BOUNDS[j + 1] - BOUNDS[j]
+        total = jnp.zeros((4 * size, T), jnp.float32)
         for k in range(16):
             row = rows_ref[k]
             col = cols_ref[k] % 4
             alive = k < offs_ref[16]
             index = ((row // 16) % 16) * 4 + row % 4
-            tile = thin_buf[index] if j == 0 else wide_buf[index, part(j - 1), :]
+            tile = thin_buf[index] if j == 0 else wide_buf[index, wide_part(j), :]
             picked = [
                 jnp.where(jnp.logical_and(col == t, alive), tile, jnp.zeros_like(tile)) for t in range(4)
             ]
@@ -289,7 +307,7 @@
                 jnp.concatenate(picked, axis=0), tiles[k], preferred_element_type=jnp.float32
             )
         for t in range(4):
-            acc[t, rows, :] = total[t * CHUNK : (t + 1) * CHUNK]
+            acc[t, rows, :] = total[t * size : (t + 1) * size]
 
     def swap_cores(p, j):
         rows = part(j)
@@ -396,7 +414,7 @@
         piece = partial[i * PIECE : (i + 1) * PIECE]
         gwp[i] = jnp.concatenate([piece[:, :128], piece[:, 128:]], axis=0).astype(jnp.bfloat16)
 
-    for step in range(1, 8):
+    for step in PLANE_STEPS:
         place, device = plane_peer(step)
         send(gwp.at[place], g1.at[here], gw_send.at[0], gw_recv.at[0], device)
     g1[here] = gwp[here]
@@ -410,12 +428,12 @@
     s1[...] = functools.reduce(lambda a, b: a + b, [g1[i].astype(jnp.float32) for i in range(8)]).astype(
         jnp.bfloat16
     )
-    for step in range(1, 8):
+    for step in Z_STEPS:
         send(s1, g2.at[z], gw_send.at[1], gw_recv.at[1], z_peer(step)[1])
     g2[z] = s1[...]
     drain(g2.at[pl.ds(0, 7)], gw_recv.at[1])
     s2[...] = functools.reduce(lambda a, b: a + b, [g2[i].astype(jnp.float32) for i in range(8)])
-    for step in range(1, 8):
+    for step in PLANE_STEPS:
         send(s2, gfin.at[here], gw_send.at[2], gw_recv.at[2], plane_peer(step)[1])
     gfin[here] = s2[...]
 
@@ -453,7 +471,7 @@
     hbm = pl.BlockSpec(memory_space=pltpu.HBM)
     f32, bf16, i32 = jnp.float32, jnp.bfloat16, jnp.int32
     dma = pltpu.SemaphoreType.DMA
-    parts = T // CHUNK
+    parts = len(BOUNDS) - 1
     grad_weight, grad_features = pl.pallas_call(
         kernel,
         out_shape=(

time: 141 us -> 139 us (0.986)
  no operation moved by 1% of the time
where the time goes in v6:
time: 139 us; the launch traced here: 138 us
  Pallas kernels  137 us (99%)
    pallas_call x1, Pallas kernels, local(): pl.pallas_call(kernel, out_shape=(jax.ShapeDtypeStruct((192, T), f32), ja...  135 us

profile of v6, /device:TPU:2, one launch (start us, length us, event | category | flops | bytes accessed | tf_op | source)
XLA Modules:
  0.0 137.8 jit_solution(15429661705004773309)
XLA Ops:
  1.3 134.6 %diffuse.1 = (f32[192,256]{1,0:T(8,128)}, bf16[192,1024]{1,0:T(8,128)(2,1)}) custom-call(s32[16]{0:T(128)} %rows_hbm.1, s32[16]{0:T(128)} %cols_hbm.1, s32[17]{0:T(128)} %offs_hbm.1, f32[1]{0:T(128)S(6)} %copy.10.heat_ref, bf16[1024,256]{1,0:T(8,128)(2,1)} %cot_hbm.1, bf16[192,1024]{1,0:T(8,128)(2,1)} %bitcast.2, bf16[192,256]{1,0:T(8,128)(2,1)} %weight_hbm.1, ...), custom_call_target="tpu_custom_call" | custom-call | flops 4800000000 | bytes 4000000 | tf_op jit(solution)/shard_map/diffuse/pallas_call | solution.py:475
  135.9 1.9 %hand_back.1 = (f32[192,256]{1,0:T(8,128)}, bf16[192,1024]{1,0:T(8,128)(2,1)}) custom-call(f32[192,256]{1,0:T(8,128)} %get-tuple-element.6.gw_in, bf16[192,1024]{1,0:T(8,128)(2,1)} %get-tuple-element.7.gf_in), custom_call_target="tpu_custom_call" | custom-call | tf_op jit(solution)/shard_map/hand_back/pallas_call | solution.py:527

commit v7 on v6

--- a/solution.py
+++ b/solution.py
@@ -61,7 +61,7 @@
 def kernel(
     rows_hbm, cols_hbm, offs_hbm, heat_ref, cot_hbm, feat_hbm, weight_hbm, tiles_hbm,
     gw_ref, gf_ref,
-    rows_ref, cols_ref, offs_ref, cot, feat, weight, tiles,
+    rows_ref, cols_ref, offs_ref, sorted_ref, ends_ref, sums, cot, feat, weight, tiles,
     wide0, thin0, wide1, thin1, own, acc, core_in, chip_out, chip_in, pair_out, pair_in, comb,
     gwp, g1, s1, g2, s2, gfin,
     load_sem, small_sem, cot_sem,
@@ -290,24 +290,44 @@
         for block in range(2):
             drain(thin_buf.at[pl.ds(0, 4)], ring_sem.at[p, 7, block])
 
+    def sort_slots():
+        keys = [jnp.where(k < offs_ref[16], cols_ref[k] % 4, 4) for k in range(16)]
+        ranks = []
+        for k in range(16):
+            rank = jnp.int32(0)
+            for q in range(16):
+                if q != k:
+                    ahead = keys[q] <= keys[k] if q < k else keys[q] < keys[k]
+                    rank = rank + jnp.where(ahead, 1, 0)
+            ranks.append(rank)
+        for place in range(16):
+            slot = jnp.int32(0)
+            for k in range(16):
+                slot = slot + jnp.where(ranks[k] == place, k, 0)
+            sorted_ref[place] = slot
+        for t in range(4):
+            below = jnp.int32(0)
+            for k in range(16):
+                below = below + jnp.where(keys[k] <= t, 1, 0)
+            ends_ref[t] = below
+
     def products(thin_buf, wide_buf, j):
         rows = part(j)
         size = BOUNDS[j + 1] - BOUNDS[j]
-        total = jnp.zeros((4 * size, T), jnp.float32)
+        total = jnp.zeros((size, T), jnp.float32)
+        sums[0, :size, :] = total
         for k in range(16):
-            row = rows_ref[k]
-            col = cols_ref[k] % 4
-            alive = k < offs_ref[16]
+            slot = sorted_ref[k] % 16
+            row = rows_ref[slot]
             index = ((row // 16) % 16) * 4 + row % 4
             tile = thin_buf[index] if j == 0 else wide_buf[index, wide_part(j), :]
-            picked = [
-                jnp.where(jnp.logical_and(col == t, alive), tile, jnp.zeros_like(tile)) for t in range(4)
-            ]
-            total = total + jnp.dot(
-                jnp.concatenate(picked, axis=0), tiles[k], preferred_element_type=jnp.float32
-            )
+            total = total + jnp.dot(tile, tiles[slot], preferred_element_type=jnp.float32)
+            sums[k + 1, :size, :] = total
         for t in range(4):
-            acc[t, rows, :] = total[t * size : (t + 1) * size]
+            upto = sums[ends_ref[t] % 17, :size, :]
+            if t > 0:
+                upto = upto - sums[ends_ref[t - 1] % 17, :size, :]
+            acc[t, rows, :] = upto
 
     def swap_cores(p, j):
         rows = part(j)
@@ -322,9 +342,10 @@
 
     for j in range(parts):
         hand_out(0, thin0, wide0, j, relay_two_near, own.at[2])
-    gather(0, thin0, wide0, FIRST_ORDER)
     for i, ref in enumerate((rows_ref, cols_ref, offs_ref)):
         drain(ref, small_sem.at[i])
+    sort_slots()
+    gather(0, thin0, wide0, FIRST_ORDER)
     drain(tiles, load_sem.at[0])
 
     def pass_on(j):
@@ -482,6 +503,8 @@
         out_specs=(vmem, vmem),
         scratch_shapes=[
             pltpu.SMEM((16,), i32), pltpu.SMEM((16,), i32), pltpu.SMEM((17,), i32),
+            pltpu.SMEM((16,), i32), pltpu.SMEM((4,), i32),
+            pltpu.VMEM((17, max(b - a for a, b in zip(BOUNDS, BOUNDS[1:])), T), f32),
             pltpu.VMEM((2, T, T), bf16),
             pltpu.VMEM((192, 1024), bf16),
             pltpu.VMEM((192, T), bf16),

time: 139 us -> 135 us (0.971)
  Pallas kernels: 137 us -> 134 us
    pallas_call x1, Pallas kernels: 135 us -> 132 us  [local(): pl.pallas_call(kernel, out_shape=(jax.ShapeDtypeStruct((192, T), f32), ja...]
where the time goes in v7:
time: 135 us
  Pallas kernels  134 us (99%)
    pallas_call x1, Pallas kernels, local(): pl.pallas_call(kernel, out_shape=(jax.ShapeDtypeStruct((192, T), f32), ja...  132 us

profile of v7, /device:TPU:2, one launch (start us, length us, event | category | flops | bytes accessed | tf_op | source)
XLA Modules:
  0.0 135.0 jit_solution(6429973203355649083)
XLA Ops:
  1.3 131.8 %diffuse.1 = (f32[192,256]{1,0:T(8,128)}, bf16[192,1024]{1,0:T(8,128)(2,1)}) custom-call(s32[16]{0:T(128)} %rows_hbm.1, s32[16]{0:T(128)} %cols_hbm.1, s32[17]{0:T(128)} %offs_hbm.1, f32[1]{0:T(128)S(6)} %copy.10.heat_ref, bf16[1024,256]{1,0:T(8,128)(2,1)} %cot_hbm.1, bf16[192,1024]{1,0:T(8,128)(2,1)} %bitcast.2, bf16[192,256]{1,0:T(8,128)(2,1)} %weight_hbm.1, ...), custom_call_target="tpu_custom_call" | custom-call | flops 4800000000 | bytes 4000000 | tf_op jit(solution)/shard_map/diffuse/pallas_call | solution.py:496
  133.0 1.9 %hand_back.1 = (f32[192,256]{1,0:T(8,128)}, bf16[192,1024]{1,0:T(8,128)(2,1)}) custom-call(f32[192,256]{1,0:T(8,128)} %get-tuple-element.6.gw_in, bf16[192,1024]{1,0:T(8,128)(2,1)} %get-tuple-element.7.gf_in), custom_call_target="tpu_custom_call" | custom-call | tf_op jit(solution)/shard_map/hand_back/pallas_call | solution.py:550

commit v8 on v7

--- a/solution.py
+++ b/solution.py
@@ -121,9 +121,6 @@
     load(rows_hbm, rows_ref, small_sem.at[0])
     load(cols_hbm, cols_ref, small_sem.at[1])
     load(offs_hbm, offs_ref, small_sem.at[2])
-    load(tiles_hbm, tiles, load_sem.at[0])
-    load(feat_hbm, feat, load_sem.at[1])
-    load(weight_hbm, weight, load_sem.at[2])
 
     barrier = pltpu.get_barrier_semaphore()
 
@@ -342,6 +339,9 @@
 
     for j in range(parts):
         hand_out(0, thin0, wide0, j, relay_two_near, own.at[2])
+    load(tiles_hbm, tiles, load_sem.at[0])
+    load(feat_hbm, feat, load_sem.at[1])
+    load(weight_hbm, weight, load_sem.at[2])
     for i, ref in enumerate((rows_ref, cols_ref, offs_ref)):
         drain(ref, small_sem.at[i])
     sort_slots()
@@ -369,10 +369,12 @@
     last_thin(0, thin0)
     products(thin0, wide0, 0)
     swap_cores(0, 0)
-    for j in range(1, parts):
+    close_first(1)
+    hand_out(1, thin1, wide1, 1, relay_two, own.at[1])
+    pass_on(0)
+    for j in range(2, parts):
         close_first(j)
         hand_out(1, thin1, wide1, j, relay_two, own.at[1])
-    pass_on(0)
     close_first(0)
     hand_out(1, thin1, wide1, 0, relay_two, own.at[1])
 
@@ -416,9 +418,9 @@
     last_thin(1, thin1)
     products(thin1, wide1, 0)
     swap_cores(1, 0)
+    pair_up(0)
     for j in range(1, parts):
         close_second(j)
-    pair_up(0)
     close_second(0)
     drain(feat, load_sem.at[1])
     drain(weight, load_sem.at[2])

time: 135 us -> 133 us (0.985)
  Pallas kernels: 134 us -> 131 us
    pallas_call x1, Pallas kernels: 132 us -> 129 us  [local(): pl.pallas_call(kernel, out_shape=(jax.ShapeDtypeStruct((192, T), f32), ja...]
where the time goes in v8:
time: 133 us; the launch traced here: 132 us
  Pallas kernels  131 us (98%)
    pallas_call x1, Pallas kernels, local(): pl.pallas_call(kernel, out_shape=(jax.ShapeDtypeStruct((192, T), f32), ja...  129 us

profile of v8, /device:TPU:2, one launch (start us, length us, event | category | flops | bytes accessed | tf_op | source)
XLA Modules:
  0.0 132.4 jit_solution(1763141397862071098)
XLA Ops:
  1.3 129.2 %diffuse.1 = (f32[192,256]{1,0:T(8,128)}, bf16[192,1024]{1,0:T(8,128)(2,1)}) custom-call(s32[16]{0:T(128)} %rows_hbm.1, s32[16]{0:T(128)} %cols_hbm.1, s32[17]{0:T(128)} %offs_hbm.1, f32[1]{0:T(128)S(6)} %copy.10.heat_ref, bf16[1024,256]{1,0:T(8,128)(2,1)} %cot_hbm.1, bf16[192,1024]{1,0:T(8,128)(2,1)} %bitcast.2, bf16[192,256]{1,0:T(8,128)(2,1)} %weight_hbm.1, ...), custom_call_target="tpu_custom_call" | custom-call | flops 4800000000 | bytes 4000000 | tf_op jit(solution)/shard_map/diffuse/pallas_call | solution.py:498
  130.5 1.9 %hand_back.1 = (f32[192,256]{1,0:T(8,128)}, bf16[192,1024]{1,0:T(8,128)(2,1)}) custom-call(f32[192,256]{1,0:T(8,128)} %get-tuple-element.6.gw_in, bf16[192,1024]{1,0:T(8,128)(2,1)} %get-tuple-element.7.gf_in), custom_call_target="tpu_custom_call" | custom-call | tf_op jit(solution)/shard_map/hand_back/pallas_call | solution.py:552

commit v9 on v8

--- a/solution.py
+++ b/solution.py
@@ -10,7 +10,7 @@
 MESH = pl.DeviceIdType.MESH
 T = 256
 THIN = 80
-BOUNDS = (0, 80, 160, 256)
+BOUNDS = (0, 80, 192, 256)
 RELAY = 64
 PLANE_STEPS = (3, 5, 1, 7, 4, 2, 6)
 Z_STEPS = (4, 3, 5, 2, 6, 1, 7)

time: 133 us -> 134 us (level)
  no operation moved by 1% of the time
where the time goes in v9:
time: 134 us; the launch traced here: 133 us
  Pallas kernels  132 us (99%)
    pallas_call x1, Pallas kernels, local(): pl.pallas_call(kernel, out_shape=(jax.ShapeDtypeStruct((192, T), f32), ja...  130 us

profile of v9, /device:TPU:2, one launch (start us, length us, event | category | flops | bytes accessed | tf_op | source)
XLA Modules:
  0.0 133.0 jit_solution(14515230565754257306)
XLA Ops:
  1.3 129.8 %diffuse.1 = (f32[192,256]{1,0:T(8,128)}, bf16[192,1024]{1,0:T(8,128)(2,1)}) custom-call(s32[16]{0:T(128)} %rows_hbm.1, s32[16]{0:T(128)} %cols_hbm.1, s32[17]{0:T(128)} %offs_hbm.1, f32[1]{0:T(128)S(6)} %copy.10.heat_ref, bf16[1024,256]{1,0:T(8,128)(2,1)} %cot_hbm.1, bf16[192,1024]{1,0:T(8,128)(2,1)} %bitcast.2, bf16[192,256]{1,0:T(8,128)(2,1)} %weight_hbm.1, ...), custom_call_target="tpu_custom_call" | custom-call | flops 4800000000 | bytes 4000000 | tf_op jit(solution)/shard_map/diffuse/pallas_call | solution.py:498
  131.1 1.9 %hand_back.1 = (f32[192,256]{1,0:T(8,128)}, bf16[192,1024]{1,0:T(8,128)(2,1)}) custom-call(f32[192,256]{1,0:T(8,128)} %get-tuple-element.6.gw_in, bf16[192,1024]{1,0:T(8,128)(2,1)} %get-tuple-element.7.gf_in), custom_call_target="tpu_custom_call" | custom-call | tf_op jit(solution)/shard_map/hand_back/pallas_call | solution.py:552
